TPU v7x, 768 devices: a whole 4x8x12 slice. The times are simulated.
768 devices in a mesh: dp: 96 (over y, z), expert: 8 (over x, core).
Axes of the slice: x: 4, y: 8, z: 12, core: 2. Of those that a mesh axis runs over, the one named last changes fastest.
Arguments:
- tokens: bfloat16 [12288, 3584], P('dp', 'expert'), may hold values from -6 to 6
- cotangent: bfloat16 [12288, 3584], P('dp', 'expert'), may hold values from -6 to 6
- slot_route: int32 [12288, 2], P('dp'), may hold values from 0 to 191, all different within a row; in each aligned block of 128 rows (0 to 127, 128 to 255, ...) at most 2 rows name the same one
- route_weight: float32 [12288, 2], P('dp'), may hold values from 0.1 to 1
- w_gate: bfloat16 [96, 3584, 1024], P('dp', 'expert'), may hold values from -0.09375 to 0.09375
- w_down: bfloat16 [96, 1024, 3584], P('dp', None, 'expert'), may hold values from -0.1875 to 0.1875
Outputs:
- mixed: bfloat16 [12288, 3584], P('dp', 'expert')
- input_grad: bfloat16 [12288, 3584], P('dp', 'expert')
- gate_grad: bfloat16 [96, 3584, 1024], P('dp', 'expert')
- down_grad: bfloat16 [96, 1024, 3584], P('dp', None, 'expert')
Inputs may be any that keep to these rules, and one draw needn't show every extreme that they name: `slot_route`: in each group of 128 tokens no slot is named by more than 2 picks, a bound that some block reaches; a token names 2 different slots.
All inputs are finite; a program needn't handle non-finite values.
Results may differ from a plain program's by a relative error of at most 0.024.
Values may be sent and summed in bfloat16 or wider, within the bound.
A program may use at most 32 MiB of HBM per device.

v0:
```python
import jax
import jax.numpy as jnp
from jax import lax
from jax.sharding import PartitionSpec as P


def from_behind(x, axis, by):
    devices = lax.axis_size(axis)
    return lax.ppermute(x, axis, [(i, (i + by) % devices) for i in range(devices)])


def move_rows(tensors):
    return (
        lax.all_to_all(tensors[0], "dp", split_axis=0, concat_axis=0, tiled=True),
        lax.all_to_all(tensors[1], "dp", split_axis=0, concat_axis=0, tiled=True),
    )


def reduce_hidden(partials):
    return lax.psum(partials.astype(jnp.bfloat16), "expert").astype(jnp.float32)


def partner_weights(tensors, half_dp):
    return from_behind((tensors[0], tensors[1]), "dp", half_dp)


def project(operand, weight, pattern_each):
    return jnp.einsum(pattern_each, operand, weight, preferred_element_type=jnp.float32)


def add_pair(first, second):
    first = lax.optimization_barrier(first)
    second = lax.optimization_barrier(second)
    return (first.astype(jnp.float32) + second.astype(jnp.float32)).astype(jnp.bfloat16)


def expert_pass(weights, slot_rows, slot_scaled):
    gate_mat, down_mat = weights
    gate_part = project(slot_rows, gate_mat, "smd,sdh->smh")
    gate_vals = reduce_hidden(gate_part[:, :, None, :])[:, :, 0]
    sig_gate = jax.nn.sigmoid(gate_vals)
    hidden_local = (gate_vals * sig_gate).astype(jnp.bfloat16)
    hidden = hidden_local[:, :, None, :][:, :, 0]
    slot_out = project(hidden, down_mat, "smh,shd->smd").astype(jnp.bfloat16)
    hidden_part = project(slot_scaled, down_mat, "smd,shd->smh")
    grad_hidden = reduce_hidden(hidden_part[:, :, None, :])[:, :, 0]
    grad_gate = (grad_hidden * sig_gate * (1.0 + gate_vals * (1.0 - sig_gate))).astype(jnp.bfloat16)
    gate_full = grad_gate[:, :, None, :][:, :, 0]
    slot_dx = project(gate_full, gate_mat, "smh,sdh->smd").astype(jnp.bfloat16)
    gate_part_grad = jnp.einsum(
        "smd,smh->sdh", slot_rows, gate_full, preferred_element_type=jnp.float32
    ).astype(jnp.bfloat16)
    down_part_grad = jnp.einsum(
        "smh,smd->shd", hidden, slot_scaled, preferred_element_type=jnp.float32
    ).astype(jnp.bfloat16)
    return (slot_out, slot_dx, gate_part_grad, down_part_grad)


def per_device(tokens, cotangent, slot_route, route_weight, w_gate, w_down):
    n_dp = lax.axis_size("dp")
    half_dp = n_dp // 2
    n_slots = 2 * n_dp
    tok_rows, width = tokens.shape
    picks = slot_route.shape[1]
    capacity = max(2, tok_rows * picks * 3 // (4 * n_dp))
    flat_slots = slot_route.reshape(-1)
    onehot = (flat_slots[:, None] == jnp.arange(n_slots, dtype=jnp.int32)[None, :]).astype(
        jnp.int32
    )
    position = jnp.sum((jnp.cumsum(onehot, axis=0) - onehot) * onehot, axis=1)
    target = flat_slots * capacity + position
    sources = jnp.repeat(tokens, picks, axis=0)
    scaled = (
        route_weight.reshape(-1, 1) * jnp.repeat(cotangent, picks, axis=0).astype(jnp.float32)
    ).astype(jnp.bfloat16)
    empty = jnp.zeros((n_slots * capacity, width), jnp.bfloat16)
    send_rows = empty.at[target].set(sources).reshape(n_dp, 2 * capacity, width)
    send_scaled = empty.at[target].set(scaled).reshape(n_dp, 2 * capacity, width)
    got_rows, got_scaled = move_rows((send_rows, send_scaled))
    home_rows = got_rows[:, :capacity].reshape(-1, width)
    home_scaled = got_scaled[:, :capacity].reshape(-1, width)
    copy_rows = got_rows[:, capacity:].reshape(-1, width)
    copy_scaled = got_scaled[:, capacity:].reshape(-1, width)
    gate_mat = w_gate[0]
    down_mat = w_down[0]
    far_gate, far_down = partner_weights((gate_mat, down_mat), half_dp)
    stacked = (jnp.stack([gate_mat, far_gate]), jnp.stack([down_mat, far_down]))
    results = expert_pass(
        stacked, jnp.stack([home_rows, copy_rows]), jnp.stack([home_scaled, copy_scaled])
    )
    slot_out, slot_dx, gate_parts, down_parts = results
    copy_out = slot_out[1]
    copy_dx = slot_dx[1]
    back_gate, back_down = partner_weights((gate_parts[1], down_parts[1]), half_dp)
    gate_grad = add_pair(gate_parts[0], back_gate)
    down_grad = add_pair(down_parts[0], back_down)
    return_out = jnp.stack(
        [slot_out[0].reshape(n_dp, capacity, width), copy_out.reshape(n_dp, capacity, width)],
        axis=1,
    )
    return_dx = jnp.stack(
        [slot_dx[0].reshape(n_dp, capacity, width), copy_dx.reshape(n_dp, capacity, width)], axis=1
    )
    back_out, back_dx = move_rows(
        (
            return_out.reshape(n_dp, 2 * capacity, width),
            return_dx.reshape(n_dp, 2 * capacity, width),
        )
    )
    picked_out = (
        back_out.reshape(-1, width)[target].astype(jnp.float32).reshape(tok_rows, picks, width)
    )
    picked_dx = (
        back_dx.reshape(-1, width)[target].astype(jnp.float32).reshape(tok_rows, picks, width)
    )
    mixed = jnp.sum(route_weight[:, :, None] * picked_out, axis=1).astype(jnp.bfloat16)
    input_grad = jnp.sum(picked_dx, axis=1).astype(jnp.bfloat16)
    return (mixed, input_grad, gate_grad[None], down_grad[None])


def solution(mesh):
    return jax.shard_map(
        per_device,
        mesh=mesh,
        in_specs=(
            P("dp", "expert"),
            P("dp", "expert"),
            P("dp", None),
            P("dp", None),
            P("dp", "expert", None),
            P("dp", None, "expert"),
        ),
        out_specs=(
            P("dp", "expert"),
            P("dp", "expert"),
            P("dp", "expert", None),
            P("dp", None, "expert"),
        ),
        check_vma=False,
    )
```

profile of v0, /device:TPU:22, one launch (start us, length us, event | category | flops | bytes accessed | tf_op | source)
XLA Modules:
  0.0 381.0 jit_solution(51484498141214408)
XLA Ops:
  7.2 0.7 broadcast_multiply_fusion
  7.9 0.8 copy.30
  8.7 0.1 eq.29
  8.8 0.1 eq.25
  9.1 0.1 mul.52
  9.3 0.2 fusion.9
  9.6 0.2 copy.33
  9.9 0.1 broadcast_in_dim.11
  10.1 0.2 reshape.119
  10.4 1.6 scatter_custom_fusion
  12.0 0.9 reshape.90
  12.8 21.8 %all-to-all-start = ((bf16[96,4,448]{2,1,0:T(4,128)(2,1)}), bf16[96,4,448]{2,1,0:T(4,128)(2,1)S(1)}, u32[]{:S(2)}, u32[]{:S(2)}) async-start(bf16[96,4,448]{2,1,0:T(4,128)(2,1)} %reshape.90), calls=%async_computation | async-start | bytes 786432 | tf_op jit(solution)/shard_map/all_to_all | solution.py:14
  34.8 0.2 broadcast_in_dim.12
  35.0 0.4 convert_element_type.90
  35.5 0.6 copy-done.1
  36.2 0.1 mul.56
  36.3 1.7 scatter_custom_fusion.1
  38.0 0.9 reshape.93
  38.8 18.6 %all-to-all-done = bf16[96,4,448]{2,1,0:T(4,128)(2,1)S(1)} async-done(((bf16[96,4,448]{2,1,0:T(4,128)(2,1)}), bf16[96,4,448]{2,1,0:T(4,128)(2,1)S(1)}, u32[]{:S(2)}, u32[]{:S(2)}) %all-to-all-start) | async-done | bytes 344096 | tf_op jit(solution)/shard_map/all_to_all | solution.py:14
  57.4 6.3 %all-to-all-start.2 = ((bf16[96,4,448]{2,1,0:T(4,128)(2,1)}), bf16[96,4,448]{2,1,0:T(4,128)(2,1)S(1)}, u32[]{:S(2)}, u32[]{:S(2)}) async-start(bf16[96,4,448]{2,1,0:T(4,128)(2,1)} %reshape.93), calls=%async_computation.2 | async-start | bytes 786432 | tf_op jit(solution)/shard_map/all_to_all | solution.py:15
  63.8 5.8 %collective-permute-start.1 = (bf16[1024,448]{0,1:T(8,128)(2,1)S(1)}, bf16[1024,448]{0,1:T(8,128)(2,1)}, u32[]{:S(2)}, u32[]{:S(2)}) collective-permute-start(bf16[1024,448]{0,1:T(8,128)(2,1)S(1)} %bitcast.56), channel_id=1, source_target_pairs={{0,384},{8,392},{16,400},{24,408},{32,416},{40,424},{48,432},{56,4... | collective-permute-start | bytes 2752520 | tf_op jit(solution)/shard_map/ppermute | solution.py:9
  69.6 4.1 %collective-permute-start = (bf16[448,1024]{1,0:T(8,128)(2,1)S(1)}, bf16[448,1024]{1,0:T(8,128)(2,1)}, u32[]{:S(2)}, u32[]{:S(2)}) collective-permute-start(bf16[448,1024]{1,0:T(8,128)(2,1)S(1)} %bitcast.57), channel_id=1, source_target_pairs={{0,384},{8,392},{16,400},{24,408},{32,416},{40,424},{48,432},{56,4... | collective-permute-start | bytes 2752520 | tf_op jit(solution)/shard_map/ppermute | solution.py:9
  73.8 0.3 fusion.31
  74.0 0.2 stack_reshape.12
  74.2 0.2 stack_reshape.13
  74.4 11.6 %all-to-all-done.2 = bf16[96,4,448]{2,1,0:T(4,128)(2,1)S(1)} async-done(((bf16[96,4,448]{2,1,0:T(4,128)(2,1)}), bf16[96,4,448]{2,1,0:T(4,128)(2,1)S(1)}, u32[]{:S(2)}, u32[]{:S(2)}) %all-to-all-start.2) | async-done | bytes 344096 | tf_op jit(solution)/shard_map/all_to_all | solution.py:15
  86.0 0.3 fusion.30
  86.3 0.2 stack_reshape.14
  86.4 0.2 stack_reshape.15
  86.7 69.9 %collective-permute-done = bf16[448,1024]{1,0:T(8,128)(2,1)} collective-permute-done((bf16[448,1024]{1,0:T(8,128)(2,1)S(1)}, bf16[448,1024]{1,0:T(8,128)(2,1)}, u32[]{:S(2)}, u32[]{:S(2)}) %collective-permute-start) | collective-permute-done | bytes 917536 | tf_op jit(solution)/shard_map/ppermute | solution.py:9
  156.6 2.6 convolution_convert_fusion.3
  159.3 2.7 convolution_convert_fusion.2
  161.9 74.8 %all-reduce.3.cloned.1.call-done = (bf16[2,192,1024]{2,1,0:T(8,128)(2,1)}, bf16[2,192,1024]{2,1,0:T(8,128)(2,1)}) async-done(((bf16[2,192,1024]{2,1,0:T(8,128)(2,1)}, bf16[2,192,1024]{2,1,0:T(8,128)(2,1)}), (bf16[2,192,1024]{2,1,0:T(8,128)(2,1)}, bf16[2,192,1024]{2,1,0:T(8,128)(2,1)})) %all-reduce.3.cloned.1.call-update) | async-done | bytes 1572880 | tf_op jit(solution)/shard_map/psum | solution.py:20
  236.7 2.2 convolution_convert_fusion.5
  239.0 2.0 convolution_convert_fusion
  241.4 1.1 copy.37
  242.4 16.5 %all-to-all-start.1 = ((bf16[96,4,448]{2,1,0:T(4,128)(2,1)}), bf16[96,4,448]{2,1,0:T(4,128)(2,1)S(1)}, u32[]{:S(2)}, u32[]{:S(2)}) async-start(bf16[96,4,448]{2,1,0:T(4,128)(2,1)} %copy.37), calls=%async_computation.1 | async-start | bytes 786432 | tf_op jit(solution)/shard_map/all_to_all | solution.py:14
  259.0 1.0 convolution_convert_fusion.1
  260.0 0.1 slice_bitcast_fusion.3
  260.2 6.1 %collective-permute-start.2 = (bf16[448,1024]{1,0:T(8,128)(2,1)S(1)}, bf16[448,1024]{1,0:T(8,128)(2,1)}, u32[]{:S(2)}, u32[]{:S(2)}) collective-permute-start(bf16[448,1024]{1,0:T(8,128)(2,1)S(1)} %get-tuple-element.13), channel_id=1, source_target_pairs={{0,384},{8,392},{16,400},{24,408},{32,416},{40,424},{48,432},{56,4... | collective-permute-start | bytes 2752520 | tf_op jit(solution)/shard_map/ppermute | solution.py:9
  266.3 1.1 slice_bitcast_fusion.1
  267.4 4.0 %collective-permute-start.3 = (bf16[1024,448]{0,1:T(8,128)(2,1)}, bf16[1024,448]{0,1:T(8,128)(2,1)}, u32[]{:S(2)}, u32[]{:S(2)}) collective-permute-start(bf16[1024,448]{0,1:T(8,128)(2,1)} %get-tuple-element.11), channel_id=1, source_target_pairs={{0,384},{8,392},{16,400},{24,408},{32,416},{40,424},{48,432},{56,4... | collective-permute-start | bytes 2752520 | tf_op jit(solution)/shard_map/ppermute | solution.py:9
  271.4 2.1 convolution_convert_fusion.4
  273.5 0.7 fusion.28
  274.2 1.0 stack_reshape_squeeze.15
  275.2 0.7 copy.41
  276.1 1.0 pad_maximum_fusion.7
  277.0 1.1 copy.42
  278.1 4.6 %all-to-all-done.1 = bf16[96,4,448]{2,1,0:T(4,128)(2,1)S(1)} async-done(((bf16[96,4,448]{2,1,0:T(4,128)(2,1)}), bf16[96,4,448]{2,1,0:T(4,128)(2,1)S(1)}, u32[]{:S(2)}, u32[]{:S(2)}) %all-to-all-start.1) | async-done | bytes 344096 | tf_op jit(solution)/shard_map/all_to_all | solution.py:14
  282.7 11.0 %all-to-all-start.3 = ((bf16[96,4,448]{2,1,0:T(4,128)(2,1)}), bf16[96,4,448]{2,1,0:T(4,128)(2,1)S(1)}, u32[]{:S(2)}, u32[]{:S(2)}) async-start(bf16[96,4,448]{2,1,0:T(4,128)(2,1)} %copy.42), calls=%async_computation.3 | async-start | bytes 786432 | tf_op jit(solution)/shard_map/all_to_all | solution.py:15
  293.7 33.2 %collective-permute-done.2 = bf16[448,1024]{1,0:T(8,128)(2,1)} collective-permute-done((bf16[448,1024]{1,0:T(8,128)(2,1)S(1)}, bf16[448,1024]{1,0:T(8,128)(2,1)}, u32[]{:S(2)}, u32[]{:S(2)}) %collective-permute-start.2) | collective-permute-done | bytes 917536 | tf_op jit(solution)/shard_map/ppermute | solution.py:9
  326.9 36.2 %collective-permute-done.3 = bf16[1024,448]{0,1:T(8,128)(2,1)} collective-permute-done((bf16[1024,448]{0,1:T(8,128)(2,1)}, bf16[1024,448]{0,1:T(8,128)(2,1)}, u32[]{:S(2)}, u32[]{:S(2)}) %collective-permute-start.3) | collective-permute-done | bytes 917536 | tf_op jit(solution)/shard_map/ppermute | solution.py:9
  363.1 2.4 fusion.7
  365.5 2.4 fusion.8
  368.0 0.2 reshape.92
  368.2 1.2 gather_fusion
  369.3 0.3 reshape.98
  369.7 0.7 multiply_reduce_fusion
  370.4 0.8 copy.43
  371.2 0.2 reshape.95
  371.4 1.2 gather_fusion.1
  372.5 0.1 gather.10
  372.7 0.7 reduce_sum.35
  373.4 0.8 copy.44
  (54 shorter events, 1.3 us)
Async XLA Ops:
  7.2 2.6 copy-start.3
  9.9 24.8 %copy-start.4 = (bf16[128,448]{0,1:T(8,128)(2,1)S(1)}, bf16[128,448]{0,1:T(8,128)(2,1)}, u32[]{:S(2)}) copy-start(bf16[128,448]{0,1:T(8,128)(2,1)} %param.7) | copy-start | bytes 344068
  12.8 22.5 %copy-start.5 = (f32[128,2]{0,1:T(2,128)S(1)}, f32[128,2]{0,1:T(2,128)}, u32[]{:S(2)}) copy-start(f32[128,2]{0,1:T(2,128)} %param.9) | copy-start | bytes 3076
  12.8 44.6 %all-to-all-start = ((bf16[96,4,448]{2,1,0:T(4,128)(2,1)}), bf16[96,4,448]{2,1,0:T(4,128)(2,1)S(1)}, u32[]{:S(2)}, u32[]{:S(2)}) async-start(bf16[96,4,448]{2,1,0:T(4,128)(2,1)} %reshape.90), calls=%async_computation | async-start | bytes 786432 | tf_op jit(solution)/shard_map/all_to_all | solution.py:14
  35.4 28.4 %copy-start.6 = (bf16[1,1024,448]{1,2,0:T(8,128)(2,1)S(1)}, bf16[1,1024,448]{1,2,0:T(8,128)(2,1)}, u32[]{:S(2)}) copy-start(bf16[1,1024,448]{1,2,0:T(8,128)(2,1)} %param.11) | copy-start | bytes 2752516
  35.4 34.2 %copy-start.7 = (bf16[1,448,1024]{2,1,0:T(8,128)(2,1)S(1)}, bf16[1,448,1024]{2,1,0:T(8,128)(2,1)}, u32[]{:S(2)}) copy-start(bf16[1,448,1024]{2,1,0:T(8,128)(2,1)} %param.10) | copy-start | bytes 2752516
  35.5 0.6 copy-start.1
  57.4 28.6 %all-to-all-start.2 = ((bf16[96,4,448]{2,1,0:T(4,128)(2,1)}), bf16[96,4,448]{2,1,0:T(4,128)(2,1)S(1)}, u32[]{:S(2)}, u32[]{:S(2)}) async-start(bf16[96,4,448]{2,1,0:T(4,128)(2,1)} %reshape.93), calls=%async_computation.2 | async-start | bytes 786432 | tf_op jit(solution)/shard_map/all_to_all | solution.py:15
  63.7 173.0 %all-reduce.3.cloned.1.call-start = ((), (), s32[]{:S(2)}) async-start(), calls=%async_computation.4 | async-start | bytes 3145728 | tf_op jit(solution)/shard_map/psum | solution.py:20
  63.8 95.5 %collective-permute-start.1 = (bf16[1024,448]{0,1:T(8,128)(2,1)S(1)}, bf16[1024,448]{0,1:T(8,128)(2,1)}, u32[]{:S(2)}, u32[]{:S(2)}) collective-permute-start(bf16[1024,448]{0,1:T(8,128)(2,1)S(1)} %bitcast.56), channel_id=1, source_target_pairs={{0,384},{8,392},{16,400},{24,408},{32,416},{40,424},{48,432},{56,4... | collective-permute-start | bytes 2752520 | tf_op jit(solution)/shard_map/ppermute | solution.py:9
  69.6 87.0 %collective-permute-start = (bf16[448,1024]{1,0:T(8,128)(2,1)S(1)}, bf16[448,1024]{1,0:T(8,128)(2,1)}, u32[]{:S(2)}, u32[]{:S(2)}) collective-permute-start(bf16[448,1024]{1,0:T(8,128)(2,1)S(1)} %bitcast.57), channel_id=1, source_target_pairs={{0,384},{8,392},{16,400},{24,408},{32,416},{40,424},{48,432},{56,4... | collective-permute-start | bytes 2752520 | tf_op jit(solution)/shard_map/ppermute | solution.py:9
  236.7 2.2 copy-start.9
  241.2 17.8 %copy-start.11 = (bf16[2,192,1024]{2,1,0:T(8,128)(2,1)S(1)}, bf16[2,192,1024]{2,1,0:T(8,128)(2,1)}, u32[]{:S(2)}) copy-start(bf16[2,192,1024]{2,1,0:T(8,128)(2,1)} %get-tuple-element.9) | copy-start | bytes 2359300
  242.4 40.3 %all-to-all-start.1 = ((bf16[96,4,448]{2,1,0:T(4,128)(2,1)}), bf16[96,4,448]{2,1,0:T(4,128)(2,1)S(1)}, u32[]{:S(2)}, u32[]{:S(2)}) async-start(bf16[96,4,448]{2,1,0:T(4,128)(2,1)} %copy.37), calls=%async_computation.1 | async-start | bytes 786432 | tf_op jit(solution)/shard_map/all_to_all | solution.py:14
  260.0 6.3 %copy-start = (bf16[2,1024,448]{1,2,0:T(8,128)(2,1)S(1)}, bf16[2,1024,448]{1,2,0:T(8,128)(2,1)}, u32[]{:S(2)}) copy-start(bf16[2,1024,448]{1,2,0:T(8,128)(2,1)} %convolution_convert_fusion) | copy-start | bytes 5505028
  260.2 11.2 %copy-start.8 = (bf16[1,448,1024]{2,1,0:T(8,128)(2,1)S(1)}, bf16[1,448,1024]{2,1,0:T(8,128)(2,1)}, u32[]{:S(2)}) copy-start(bf16[1,448,1024]{2,1,0:T(8,128)(2,1)} %param.10) | copy-start | bytes 2752516
  260.2 11.2 %copy-start.10 = (bf16[2,192,1024]{2,1,0:T(8,128)(2,1)S(1)}, bf16[2,192,1024]{2,1,0:T(8,128)(2,1)}, u32[]{:S(2)}) copy-start(bf16[2,192,1024]{2,1,0:T(8,128)(2,1)} %get-tuple-element.8) | copy-start | bytes 2359300
  260.2 11.2 %copy-start.12 = (bf16[2,192,1024]{2,1,0:T(8,128)(2,1)S(1)}, bf16[2,192,1024]{2,1,0:T(8,128)(2,1)}, u32[]{:S(2)}) copy-start(bf16[2,192,1024]{2,1,0:T(8,128)(2,1)} %get-tuple-element.9) | copy-start | bytes 2359300
  260.2 66.7 %collective-permute-start.2 = (bf16[448,1024]{1,0:T(8,128)(2,1)S(1)}, bf16[448,1024]{1,0:T(8,128)(2,1)}, u32[]{:S(2)}, u32[]{:S(2)}) collective-permute-start(bf16[448,1024]{1,0:T(8,128)(2,1)S(1)} %get-tuple-element.13), channel_id=1, source_target_pairs={{0,384},{8,392},{16,400},{24,408},{32,416},{40,424},{48,432},{56,4... | collective-permute-start | bytes 2752520 | tf_op jit(solution)/shard_map/ppermute | solution.py:9
  267.4 95.7 %collective-permute-start.3 = (bf16[1024,448]{0,1:T(8,128)(2,1)}, bf16[1024,448]{0,1:T(8,128)(2,1)}, u32[]{:S(2)}, u32[]{:S(2)}) collective-permute-start(bf16[1024,448]{0,1:T(8,128)(2,1)} %get-tuple-element.11), channel_id=1, source_target_pairs={{0,384},{8,392},{16,400},{24,408},{32,416},{40,424},{48,432},{56,4... | collective-permute-start | bytes 2752520 | tf_op jit(solution)/shard_map/ppermute | solution.py:9
  282.7 88.5 %all-to-all-start.3 = ((bf16[96,4,448]{2,1,0:T(4,128)(2,1)}), bf16[96,4,448]{2,1,0:T(4,128)(2,1)S(1)}, u32[]{:S(2)}, u32[]{:S(2)}) async-start(bf16[96,4,448]{2,1,0:T(4,128)(2,1)} %copy.42), calls=%async_computation.3 | async-start | bytes 786432 | tf_op jit(solution)/shard_map/all_to_all | solution.py:15
  368.2 1.5 copy-start.2
Sparse Core Ops, SparseCore 0:
  162.1 74.6 all-reduce.2
where the time goes:
time: 382 us; the launch traced here: 381 us
  waiting for transfers between devices  249 us (65%)
  starting transfers between devices  75.7 us (20%)
  local copies, waits for them, and re-layouts  19 us (5%)
  between operations  14.6 us (4%)
  matrix products  12.7 us (3%)
  other arithmetic  10.1 us (3%)
    ppermute x4, waiting for transfers between devices, from_behind(): lax.ppermute(x, axis, [(i, (i + by) % devices) for i in range(devices)])  139 us
    psum x1, waiting for transfers between devices, reduce_hidden(): return lax.psum(partials.astype(jnp.bfloat16), 'expert').astype(jnp.float32)  74.8 us
    all_to_all x2, starting transfers between devices, move_rows(): lax.all_to_all(tensors[0], 'dp', split_axis=0, concat_axis=0, tiled=True)  38.4 us
    all_to_all x2, waiting for transfers between devices, move_rows(): lax.all_to_all(tensors[0], 'dp', split_axis=0, concat_axis=0, tiled=True)  23.2 us
    ppermute x4, starting transfers between devices, from_behind(): lax.ppermute(x, axis, [(i, (i + by) % devices) for i in range(devices)])  20 us
    all_to_all x2, starting transfers between devices, move_rows(): lax.all_to_all(tensors[1], 'dp', split_axis=0, concat_axis=0, tiled=True)  17.3 us
    all_to_all x2, waiting for transfers between devices, move_rows(): lax.all_to_all(tensors[1], 'dp', split_axis=0, concat_axis=0, tiled=True)  11.6 us
    dot_general x4, matrix products, project(): jnp.einsum(pattern_each, operand, weight, preferred_element_type=jnp.floa...  9.61 us
  transfers between devices with their start and end apart: 9, of which 7 were waited for; matrix products, arithmetic and copies ran while one was open for 6% of the time, Pallas kernels for 0%

commit v1 on v0

v1 whole, which is shorter than its diff:
```python
import jax
import jax.numpy as jnp
from jax import lax
from jax.sharding import PartitionSpec as P


def move_rows(tensors):
    return (
        lax.all_to_all(tensors[0], "dp", split_axis=0, concat_axis=0, tiled=True),
        lax.all_to_all(tensors[1], "dp", split_axis=0, concat_axis=0, tiled=True),
    )


def reduce_hidden(partials):
    return lax.psum(partials.astype(jnp.bfloat16), "expert").astype(jnp.float32)


def project(operand, weight, pattern_each):
    return jnp.einsum(pattern_each, operand, weight, preferred_element_type=jnp.float32)


def expert_pass(weights, slot_rows, slot_scaled):
    gate_mat, down_mat = weights
    gate_part = project(slot_rows, gate_mat, "md,dh->mh")
    gate_vals = reduce_hidden(gate_part)
    sig_gate = jax.nn.sigmoid(gate_vals)
    hidden_local = (gate_vals * sig_gate).astype(jnp.bfloat16)
    hidden = hidden_local
    slot_out = project(hidden, down_mat, "mh,hd->md").astype(jnp.bfloat16)
    hidden_part = project(slot_scaled, down_mat, "md,hd->mh")
    grad_hidden = reduce_hidden(hidden_part)
    grad_gate = (grad_hidden * sig_gate * (1.0 + gate_vals * (1.0 - sig_gate))).astype(jnp.bfloat16)
    gate_full = grad_gate
    slot_dx = project(gate_full, gate_mat, "mh,dh->md").astype(jnp.bfloat16)
    gate_part_grad = jnp.einsum(
        "md,mh->dh", slot_rows, gate_full, preferred_element_type=jnp.float32
    ).astype(jnp.bfloat16)
    down_part_grad = jnp.einsum(
        "mh,md->hd", hidden, slot_scaled, preferred_element_type=jnp.float32
    ).astype(jnp.bfloat16)
    return (slot_out, slot_dx, gate_part_grad, down_part_grad)


def per_device(tokens, cotangent, slot_route, route_weight, w_gate, w_down):
    n_dp = lax.axis_size("dp")
    half_dp = n_dp // 2
    n_slots = 2 * n_dp
    tok_rows, width = tokens.shape
    picks = slot_route.shape[1]
    capacity = max(2, tok_rows * picks * 3 // (4 * n_dp))
    flat_slots = slot_route.reshape(-1)
    onehot = (flat_slots[:, None] == jnp.arange(n_slots, dtype=jnp.int32)[None, :]).astype(
        jnp.int32
    )
    position = jnp.sum((jnp.cumsum(onehot, axis=0) - onehot) * onehot, axis=1)
    pair = flat_slots // 2
    odd = flat_slots % 2
    home = jnp.where(odd == 1, (pair + half_dp) % n_dp, pair)
    target = (home * 2 + odd) * capacity + position
    sources = jnp.repeat(tokens, picks, axis=0)
    scaled = (
        route_weight.reshape(-1, 1) * jnp.repeat(cotangent, picks, axis=0).astype(jnp.float32)
    ).astype(jnp.bfloat16)
    empty = jnp.zeros((n_slots * capacity, width), jnp.bfloat16)
    send_rows = empty.at[target].set(sources).reshape(n_dp, 2 * capacity, width)
    send_scaled = empty.at[target].set(scaled).reshape(n_dp, 2 * capacity, width)
    got_rows, got_scaled = move_rows((send_rows, send_scaled))
    results = expert_pass(
        (w_gate[0], w_down[0]), got_rows.reshape(-1, width), got_scaled.reshape(-1, width)
    )
    slot_out, slot_dx, gate_grad, down_grad = results
    back_out, back_dx = move_rows(
        (
            slot_out.reshape(n_dp, 2 * capacity, width),
            slot_dx.reshape(n_dp, 2 * capacity, width),
        )
    )
    picked_out = (
        back_out.reshape(-1, width)[target].astype(jnp.float32).reshape(tok_rows, picks, width)
    )
    picked_dx = (
        back_dx.reshape(-1, width)[target].astype(jnp.float32).reshape(tok_rows, picks, width)
    )
    mixed = jnp.sum(route_weight[:, :, None] * picked_out, axis=1).astype(jnp.bfloat16)
    input_grad = jnp.sum(picked_dx, axis=1).astype(jnp.bfloat16)
    return (mixed, input_grad, gate_grad[None], down_grad[None])


def solution(mesh):
    return jax.shard_map(
        per_device,
        mesh=mesh,
        in_specs=(
            P("dp", "expert"),
            P("dp", "expert"),
            P("dp", None),
            P("dp", None),
            P("dp", "expert", None),
            P("dp", None, "expert"),
        ),
        out_specs=(
            P("dp", "expert"),
            P("dp", "expert"),
            P("dp", "expert", None),
            P("dp", None, "expert"),
        ),
        check_vma=False,
    )
```

time: 382 us -> 241 us (0.63)
  the two profiles are of different devices: /device:TPU:22 before, /device:TPU:14 now
where the time goes in v1:
time: 241 us
  waiting for transfers between devices  146 us (61%)
  starting transfers between devices  50.9 us (21%)
  local copies, waits for them, and re-layouts  14.4 us (6%)
  between operations  14.3 us (6%)
  matrix products  9.55 us (4%)
  other arithmetic  5.48 us (2%)
    psum x1, waiting for transfers between devices, reduce_hidden(): return lax.psum(partials.astype(jnp.bfloat16), 'expert').astype(jnp.float32)  69.1 us
    all_to_all x2, waiting for transfers between devices, move_rows(): lax.all_to_all(tensors[1], 'dp', split_axis=0, concat_axis=0, tiled=True)  39.4 us
    all_to_all x2, starting transfers between devices, move_rows(): lax.all_to_all(tensors[1], 'dp', split_axis=0, concat_axis=0, tiled=True)  38.3 us
    all_to_all x2, waiting for transfers between devices, move_rows(): lax.all_to_all(tensors[0], 'dp', split_axis=0, concat_axis=0, tiled=True)  37.3 us
    all_to_all x2, starting transfers between devices, move_rows(): lax.all_to_all(tensors[0], 'dp', split_axis=0, concat_axis=0, tiled=True)  12.6 us
    dot_general x4, matrix products, project(): jnp.einsum(pattern_each, operand, weight, preferred_element_type=jnp.floa...  6.22 us
  transfers between devices with their start and end apart: 5, of which 5 were waited for; matrix products, arithmetic and copies ran while one was open for 6% of the time, Pallas kernels for 0%

profile of v1, /device:TPU:14, one launch (start us, length us, event | category | flops | bytes accessed | tf_op | source)
XLA Modules:
  0.0 240.5 jit_solution(4725767947835200889)
XLA Ops:
  7.2 0.0 copy-start
  7.2 0.0 copy-start.7
  7.2 0.0 copy-start.5
  7.2 0.9 copy.27
  8.1 0.1 eq.44
  8.2 0.1 eq.40
  8.4 0.1 reshape.213
  8.5 0.1 copy.30
  8.6 0.2 fusion.13
  8.9 0.2 copy.31
  9.1 0.0 copy-done.7
  9.1 0.1 copy.26
  9.2 0.1 mul.59
  9.3 0.1 copy.35
  9.5 0.2 broadcast_in_dim.23
  9.6 0.4 convert_element_type.70
  10.0 0.1 fusion.19
  10.1 1.7 scatter_custom_fusion.1
  11.8 0.0 copy-start.6
  11.8 0.9 reshape.220
  12.7 21.8 %all-to-all-start.2 = ((bf16[96,4,448]{2,1,0:T(4,128)(2,1)}), bf16[96,4,448]{2,1,0:T(4,128)(2,1)S(1)}, u32[]{:S(2)}, u32[]{:S(2)}) async-start(bf16[96,4,448]{2,1,0:T(4,128)(2,1)} %reshape.220), calls=%async_computation.2 | async-start | bytes 786432 | tf_op jit(solution)/shard_map/all_to_all | solution.py:10
  34.5 0.1 copy.32
  34.6 0.1 broadcast_in_dim.22
  34.7 0.2 reshape.245
  34.9 1.6 scatter_custom_fusion
  36.6 0.9 reshape.216
  37.4 19.9 %all-to-all-done.2 = bf16[96,4,448]{2,1,0:T(4,128)(2,1)S(1)} async-done(((bf16[96,4,448]{2,1,0:T(4,128)(2,1)}), bf16[96,4,448]{2,1,0:T(4,128)(2,1)S(1)}, u32[]{:S(2)}, u32[]{:S(2)}) %all-to-all-start.2) | async-done | bytes 344096 | tf_op jit(solution)/shard_map/all_to_all | solution.py:10
  57.3 6.2 %all-to-all-start = ((bf16[96,4,448]{2,1,0:T(4,128)(2,1)}), bf16[96,4,448]{2,1,0:T(4,128)(2,1)S(1)}, u32[]{:S(2)}, u32[]{:S(2)}) async-start(bf16[96,4,448]{2,1,0:T(4,128)(2,1)} %reshape.216), calls=%async_computation | async-start | bytes 786432 | tf_op jit(solution)/shard_map/all_to_all | solution.py:9
  63.5 0.0 all-reduce.3.cloned.1.call-start
  63.6 0.2 reshape.221
  63.8 1.5 convolution_convert_fusion.2
  65.2 0.0 copy-done.3
  65.3 20.7 %all-to-all-done = bf16[96,4,448]{2,1,0:T(4,128)(2,1)S(1)} async-done(((bf16[96,4,448]{2,1,0:T(4,128)(2,1)}), bf16[96,4,448]{2,1,0:T(4,128)(2,1)S(1)}, u32[]{:S(2)}, u32[]{:S(2)}) %all-to-all-start) | async-done | bytes 344096 | tf_op jit(solution)/shard_map/all_to_all | solution.py:9
  85.9 0.2 reshape.217
  86.1 1.5 convolution_convert_fusion.3
  87.6 0.0 all-reduce.3.cloned.1.call-update
  87.6 69.1 %all-reduce.3.cloned.1.call-done = (bf16[384,1024]{1,0:T(8,128)(2,1)}, bf16[384,1024]{1,0:T(8,128)(2,1)}) async-done(((bf16[384,1024]{1,0:T(8,128)(2,1)}, bf16[384,1024]{1,0:T(8,128)(2,1)}), (bf16[384,1024]{1,0:T(8,128)(2,1)}, bf16[384,1024]{1,0:T(8,128)(2,1)})) %all-reduce.3.cloned.1.call-update) | async-done | bytes 1572880 | tf_op jit(solution)/shard_map/psum | solution.py:15
  156.7 2.0 fusion.6
  158.7 0.7 convolution_convert_fusion.4
  159.4 0.2 copy.36
  159.6 0.0 copy-start.1
  159.6 0.9 reshape.222
  160.5 16.5 %all-to-all-start.3 = ((bf16[96,4,448]{2,1,0:T(4,128)(2,1)}), bf16[96,4,448]{2,1,0:T(4,128)(2,1)S(1)}, u32[]{:S(2)}, u32[]{:S(2)}) async-start(bf16[96,4,448]{2,1,0:T(4,128)(2,1)} %reshape.222), calls=%async_computation.3 | async-start | bytes 786432 | tf_op jit(solution)/shard_map/all_to_all | solution.py:10
  177.0 0.0 copy-done.1
  177.0 2.6 %convolution_convert_fusion.5 = bf16[384,448]{0,1:T(8,128)(2,1)} fusion(bf16[1,1024,448]{1,2,0:T(8,128)(2,1)} %param.11, bf16[384,1024]{1,0:T(8,128)(2,1)S(1)} %copy-done.1), kind=kOutput, calls=%fused_computation.21 | convolution fusion | flops 354852864 | bytes 2048000 | tf_op jit(solution)/shard_map/mh,hd->md/dot_general | solution.py:19
  179.6 1.1 copy.33
  180.8 0.8 reshape.218
  181.6 19.5 %all-to-all-done.3 = bf16[96,4,448]{2,1,0:T(4,128)(2,1)S(1)} async-done(((bf16[96,4,448]{2,1,0:T(4,128)(2,1)}), bf16[96,4,448]{2,1,0:T(4,128)(2,1)S(1)}, u32[]{:S(2)}, u32[]{:S(2)}) %all-to-all-start.3) | async-done | bytes 344096 | tf_op jit(solution)/shard_map/all_to_all | solution.py:10
  201.1 6.4 %all-to-all-start.1 = ((bf16[96,4,448]{2,1,0:T(4,128)(2,1)}), bf16[96,4,448]{2,1,0:T(4,128)(2,1)S(1)}, u32[]{:S(2)}, u32[]{:S(2)}) async-start(bf16[96,4,448]{2,1,0:T(4,128)(2,1)} %reshape.218), calls=%async_computation.1 | async-start | bytes 786432 | tf_op jit(solution)/shard_map/all_to_all | solution.py:9
  207.6 0.0 copy-start.2
  207.6 0.0 copy-start.4
  207.6 1.6 fusion.7
  209.2 1.7 fusion.8
  210.9 0.2 reshape.223
  211.1 1.2 gather_fusion.1
  212.3 0.1 gather.10
  212.4 0.7 reduce_sum.35
  213.1 0.8 copy.38
  213.9 16.6 %all-to-all-done.1 = bf16[96,4,448]{2,1,0:T(4,128)(2,1)S(1)} async-done(((bf16[96,4,448]{2,1,0:T(4,128)(2,1)}), bf16[96,4,448]{2,1,0:T(4,128)(2,1)S(1)}, u32[]{:S(2)}, u32[]{:S(2)}) %all-to-all-start.1) | async-done | bytes 344096 | tf_op jit(solution)/shard_map/all_to_all | solution.py:9
  230.5 0.2 reshape.219
  230.7 1.2 gather_fusion
  231.8 0.3 reshape.224
  232.2 0.7 multiply_reduce_fusion
  232.9 0.8 copy.37
  (15 shorter events, 0.1 us)
Async XLA Ops:
  7.2 78.9 %copy-start = (bf16[1,448,1024]{2,1,0:T(8,128)(2,1)S(1)}, bf16[1,448,1024]{2,1,0:T(8,128)(2,1)}, u32[]{:S(2)}) copy-start(bf16[1,448,1024]{2,1,0:T(8,128)(2,1)} %param.10) | copy-start | bytes 2752516
  7.2 1.9 copy-start.7
  7.2 2.1 copy-start.5
  11.8 22.7 %copy-start.6 = (bf16[128,448]{0,1:T(8,128)(2,1)S(1)}, bf16[128,448]{0,1:T(8,128)(2,1)}, u32[]{:S(2)}) copy-start(bf16[128,448]{0,1:T(8,128)(2,1)} %param.6) | copy-start | bytes 344068
  12.7 44.7 %all-to-all-start.2 = ((bf16[96,4,448]{2,1,0:T(4,128)(2,1)}), bf16[96,4,448]{2,1,0:T(4,128)(2,1)S(1)}, u32[]{:S(2)}, u32[]{:S(2)}) async-start(bf16[96,4,448]{2,1,0:T(4,128)(2,1)} %reshape.220), calls=%async_computation.2 | async-start | bytes 786432 | tf_op jit(solution)/shard_map/all_to_all | solution.py:10
  37.4 26.4 %copy-start.8 = (bf16[1,1024,448]{1,2,0:T(8,128)(2,1)S(1)}, bf16[1,1024,448]{1,2,0:T(8,128)(2,1)}, u32[]{:S(2)}) copy-start(bf16[1,1024,448]{1,2,0:T(8,128)(2,1)} %param.11) | copy-start | bytes 2752516
  57.3 28.6 %all-to-all-start = ((bf16[96,4,448]{2,1,0:T(4,128)(2,1)}), bf16[96,4,448]{2,1,0:T(4,128)(2,1)S(1)}, u32[]{:S(2)}, u32[]{:S(2)}) async-start(bf16[96,4,448]{2,1,0:T(4,128)(2,1)} %reshape.216), calls=%async_computation | async-start | bytes 786432 | tf_op jit(solution)/shard_map/all_to_all | solution.py:9
  63.5 93.2 %all-reduce.3.cloned.1.call-start = ((), (), s32[]{:S(2)}) async-start(), calls=%async_computation.4 | async-start | bytes 3145728 | tf_op jit(solution)/shard_map/psum | solution.py:15
  63.8 1.5 copy-start.3
  159.6 17.4 %copy-start.1 = (bf16[384,1024]{1,0:T(8,128)(2,1)S(1)}, bf16[384,1024]{1,0:T(8,128)(2,1)}, u32[]{:S(2)}) copy-start(bf16[384,1024]{1,0:T(8,128)(2,1)} %get-tuple-element.8) | copy-start | bytes 2359300
  160.5 40.6 %all-to-all-start.3 = ((bf16[96,4,448]{2,1,0:T(4,128)(2,1)}), bf16[96,4,448]{2,1,0:T(4,128)(2,1)S(1)}, u32[]{:S(2)}, u32[]{:S(2)}) async-start(bf16[96,4,448]{2,1,0:T(4,128)(2,1)} %reshape.222), calls=%async_computation.3 | async-start | bytes 786432 | tf_op jit(solution)/shard_map/all_to_all | solution.py:10
  201.1 29.4 %all-to-all-start.1 = ((bf16[96,4,448]{2,1,0:T(4,128)(2,1)}), bf16[96,4,448]{2,1,0:T(4,128)(2,1)S(1)}, u32[]{:S(2)}, u32[]{:S(2)}) async-start(bf16[96,4,448]{2,1,0:T(4,128)(2,1)} %reshape.218), calls=%async_computation.1 | async-start | bytes 786432 | tf_op jit(solution)/shard_map/all_to_all | solution.py:9
  207.6 1.6 copy-start.2
  207.6 1.6 copy-start.4
Sparse Core Ops, SparseCore 0:
  87.7 68.9 all-reduce.2

commit v2 on v1

v2 whole, which is shorter than its diff:
```python
import jax
import jax.numpy as jnp
from jax import lax
from jax.experimental import pallas as pl
from jax.experimental.pallas import tpu as pltpu
from jax.sharding import PartitionSpec as P

NY, NZ, NX, NCORE = 8, 12, 4, 2
BF16, F32 = jnp.bfloat16, jnp.float32
TOK = 128
WIDTH = 448
LANES = 2 * WIDTH
ROWS = 2 * NY * NZ
HW = 1024
PART = ROWS // NX
PAD = 64
TILE = 512


def spread(k, n):
    return n // 2 + (k // 2) * (1 - 2 * (k % 2))


def dot(a, b, contract_a=1, contract_b=0):
    return lax.dot_general(a, b, (((contract_a,), (contract_b,)), ((), ())), preferred_element_type=F32)


def layer(
    tok_hbm, cot_hbm, slot_ref, weight_ref, gate_hbm, down_hbm,
    mixed_ref, grad_ref, gate_grad_hbm, down_grad_hbm,
    tok_src, cot_src, gate_w, down_w, pick, perm_out, perm_back,
    z_out, z_in, y_out, y_in, rows,
    core_out, core_in, own, x_out, x_in, hid, gate_keep,
    yb_out, yb_in, zb_out, zb_in, grad_w,
    load_sem, store_sem,
    z_send, z_recv, y_send, y_recv, c_send, c_recv, x_send, x_recv,
    g_send, g_recv, f_send, f_recv, yb_send, yb_recv, zb_send, zb_recv,
):
    dp, ex = lax.axis_index("dp"), lax.axis_index("expert")
    y, z = dp // NZ, dp % NZ
    x, core = ex // NCORE, ex % NCORE
    other = 1 - core

    def at_z(k):
        return (y * NZ + (z + spread(k, NZ)) % NZ, ex)

    def at_y(k):
        return (((y + spread(k, NY)) % NY) * NZ + z, ex)

    def at_x(k):
        return (dp, ((x + spread(k, NX)) % NX) * NCORE + core)

    at_core = (dp, x * NCORE + other)

    loads = [
        pltpu.make_async_copy(tok_hbm, tok_src.at[pl.ds(0, WIDTH), pl.ds(0, TOK)], load_sem.at[0]),
        pltpu.make_async_copy(tok_hbm, tok_src.at[pl.ds(WIDTH, WIDTH), pl.ds(TOK, TOK)], load_sem.at[1]),
        pltpu.make_async_copy(cot_hbm, cot_src.at[pl.ds(0, WIDTH), pl.ds(0, TOK)], load_sem.at[2]),
        pltpu.make_async_copy(cot_hbm, cot_src.at[pl.ds(WIDTH, WIDTH), pl.ds(TOK, TOK)], load_sem.at[3]),
        pltpu.make_async_copy(gate_hbm, gate_w.at[pl.ds(PAD, WIDTH)], load_sem.at[4]),
        pltpu.make_async_copy(down_hbm, down_w.at[pl.ds(PAD, WIDTH)], load_sem.at[5]),
    ]
    for load in loads:
        load.start()

    barrier = pltpu.get_barrier_semaphore()

    def hello(place, count):
        def one(k, carry):
            pl.semaphore_signal(barrier, inc=1, device_id=place(k), device_id_type=pl.DeviceIdType.MESH)
            return carry

        lax.fori_loop(1, count, one, 0)

    hello(at_z, NZ)
    hello(at_y, NY)
    hello(at_x, NX)
    pl.semaphore_signal(barrier, inc=1, device_id=at_core, device_id_type=pl.DeviceIdType.MESH)

    j = lax.broadcasted_iota(jnp.int32, (ROWS, TOK), 0)
    to = ((j >> 1) & (NY - 1)) * NZ + (j >> 4)
    half = NY * NZ // 2
    slot = jnp.where((j & 1) == 1, 2 * jnp.where(to < half, to + half, to - half) + 1, 2 * to)
    is_0, is_1 = slot == slot_ref[0:1, :], slot == slot_ref[1:2, :]
    named = jnp.where(is_0 | is_1, 1.0, 0.0)
    earlier = lax.broadcasted_iota(jnp.int32, (TOK, TOK), 0) < lax.broadcasted_iota(jnp.int32, (TOK, TOK), 1)
    before = dot(named.astype(BF16), jnp.where(earlier, 1.0, 0.0).astype(BF16))
    first = jnp.where(before < 0.5, 1.0, 0.0)
    later = 1.0 - first
    one_0, one_1 = jnp.where(is_0, 1.0, 0.0), jnp.where(is_1, 1.0, 0.0)
    pick[0] = jnp.concatenate([one_0 * first, one_1 * first], axis=1).astype(BF16)
    pick[1] = jnp.concatenate([one_0 * later, one_1 * later], axis=1).astype(BF16)
    chosen = jnp.concatenate([named * first, named * later], axis=1).astype(BF16)
    weight_of = one_0 * weight_ref[0:1, :] + one_1 * weight_ref[1:2, :]
    scale_first = jnp.sum(weight_of * first, axis=1, keepdims=True)
    scale_later = jnp.sum(weight_of * later, axis=1, keepdims=True)
    lane = lax.broadcasted_iota(jnp.int32, (ROWS, LANES), 1)
    scale = jnp.where(lane < WIDTH, scale_first, scale_later)

    down_axis = lax.broadcasted_iota(jnp.int32, (ROWS, ROWS), 0)
    along_axis = lax.broadcasted_iota(jnp.int32, (ROWS, ROWS), 1)

    def place(c):
        return ((c >> 1) & (NY - 1)) * (2 * NZ) + (c >> 4) * 2 + (c & 1)

    perm_out[...] = jnp.where(down_axis == place(along_axis), 1.0, 0.0).astype(BF16)
    perm_back[...] = jnp.where(place(down_axis) == along_axis, 1.0, 0.0).astype(BF16)

    for src in (tok_src, cot_src):
        src[pl.ds(0, WIDTH), pl.ds(TOK, TOK)] = jnp.zeros((WIDTH, TOK), BF16)
        src[pl.ds(WIDTH, WIDTH), pl.ds(0, TOK)] = jnp.zeros((WIDTH, TOK), BF16)
    for mat in (gate_w, down_w):
        mat[pl.ds(0, PAD), :] = jnp.zeros((PAD, HW), BF16)
        mat[pl.ds(PAD + WIDTH, PAD), :] = jnp.zeros((PAD, HW), BF16)

    def z_copy(src, dst, send, recv, a, k):
        off = spread(k, NZ)
        return pltpu.make_async_remote_copy(
            src_ref=src.at[a, (z + off) % NZ], dst_ref=dst.at[a, z], send_sem=send.at[a, off],
            recv_sem=recv.at[a, off], device_id=at_z(k), device_id_type=pl.DeviceIdType.MESH)

    def z_come(src, dst, send, recv, a, k):
        off = spread(k, NZ)
        return pltpu.make_async_remote_copy(
            src_ref=src.at[a, z], dst_ref=dst.at[a, (z + NZ - off) % NZ], send_sem=send.at[a, off],
            recv_sem=recv.at[a, off], device_id=at_z(k), device_id_type=pl.DeviceIdType.MESH)

    def y_copy(src, dst, send, recv, a, k):
        off = spread(k, NY)
        return pltpu.make_async_remote_copy(
            src_ref=src.at[a, (y + off) % NY], dst_ref=dst.at[a, y], send_sem=send.at[a, off],
            recv_sem=recv.at[a, off], device_id=at_y(k), device_id_type=pl.DeviceIdType.MESH)

    def y_come(src, dst, send, recv, a, k):
        off = spread(k, NY)
        return pltpu.make_async_remote_copy(
            src_ref=src.at[a, y], dst_ref=dst.at[a, (y + NY - off) % NY], send_sem=send.at[a, off],
            recv_sem=recv.at[a, off], device_id=at_y(k), device_id_type=pl.DeviceIdType.MESH)

    def x_copy(a, k):
        off = spread(k, NX)
        return pltpu.make_async_remote_copy(
            src_ref=x_out.at[a, (x + off) % NX], dst_ref=x_in.at[a, x], send_sem=x_send.at[a, off],
            recv_sem=x_recv.at[a, off], device_id=at_x(k), device_id_type=pl.DeviceIdType.MESH)

    def x_come(a, k):
        off = spread(k, NX)
        return pltpu.make_async_remote_copy(
            src_ref=x_out.at[a, x], dst_ref=x_in.at[a, (x + NX - off) % NX], send_sem=x_send.at[a, off],
            recv_sem=x_recv.at[a, off], device_id=at_x(k), device_id_type=pl.DeviceIdType.MESH)

    def g_copy(a, k):
        off = spread(k, NX)
        return pltpu.make_async_remote_copy(
            src_ref=hid.at[a, core, x], dst_ref=hid.at[a, core, x], send_sem=g_send.at[a, off],
            recv_sem=g_recv.at[a, off], device_id=at_x(k), device_id_type=pl.DeviceIdType.MESH)

    def g_come(a, k):
        off = spread(k, NX)
        frm = (x + NX - off) % NX
        return pltpu.make_async_remote_copy(
            src_ref=hid.at[a, core, x], dst_ref=hid.at[a, core, frm], send_sem=g_send.at[a, off],
            recv_sem=g_recv.at[a, off], device_id=at_x(k), device_id_type=pl.DeviceIdType.MESH)

    def f_copy(a, off):
        frm = (x + NX - off) % NX
        return pltpu.make_async_remote_copy(
            src_ref=hid.at[a, core, frm], dst_ref=hid.at[a, core, frm], send_sem=f_send.at[a, off],
            recv_sem=f_recv.at[a, off], device_id=at_core, device_id_type=pl.DeviceIdType.MESH)

    def f_come(a, off):
        frm = (x + NX - off) % NX
        return pltpu.make_async_remote_copy(
            src_ref=hid.at[a, core, frm], dst_ref=hid.at[a, other, frm], send_sem=f_send.at[a, off],
            recv_sem=f_recv.at[a, off], device_id=at_core, device_id_type=pl.DeviceIdType.MESH)

    def c_copy(a):
        return pltpu.make_async_remote_copy(
            src_ref=core_out.at[a], dst_ref=core_in.at[a], send_sem=c_send.at[a],
            recv_sem=c_recv.at[a], device_id=at_core, device_id_type=pl.DeviceIdType.MESH)

    def each(n, step):
        def one(k, carry):
            step(k)
            return carry

        lax.fori_loop(1, n, one, 0)

    def send_z(src, dst, send, recv, a):
        each(NZ, lambda k: z_copy(src, dst, send, recv, a, k).start())
        dst[a, z] = src[a, z]

    def take_z(src, dst, send, recv, a):
        each(NZ, lambda k: z_come(src, dst, send, recv, a, k).wait_recv())
        return dst[a].reshape(ROWS, LANES)

    def send_y(value, src, dst, send, recv, a):
        for i in range(NY):
            src[a, i] = value[i * 2 * NZ:(i + 1) * 2 * NZ].astype(BF16)
        each(NY, lambda k: y_copy(src, dst, send, recv, a, k).start())
        dst[a, y] = src[a, y]

    def take_y(src, dst, send, recv, a):
        each(NY, lambda k: y_come(src, dst, send, recv, a, k).wait_recv())
        return jnp.concatenate([dst[a, i].astype(F32) for i in range(NY)], axis=0).astype(BF16)

    def project_in(a, mat, p):
        lanes = pl.ds(pl.multiple_of(p * (LANES - TILE), 128), TILE)
        deep = pl.ds(pl.multiple_of((1 - p) * PAD, PAD), TILE)
        return dot(rows[a, :, lanes], mat[deep, :])

    def start_sum(a, mat):
        core_out[a] = project_in(a, mat, other).astype(BF16)
        c_copy(a).start()
        own[a] = project_in(a, mat, core)

    def next_sum(a):
        c_copy(a).wait_recv()
        total = own[a] + core_in[a].astype(F32)
        own[a] = total
        x_out[a] = total.astype(BF16).reshape(NX, PART, HW)
        each(NX, lambda k: x_copy(a, k).start())

    def end_sum(a):
        each(NX, lambda k: x_come(a, k).wait_recv())
        total = own[a, pl.ds(pl.multiple_of(x * PART, PART), PART), :]
        for off in range(1, NX):
            total = total + x_in[a, (x + NX - off) % NX].astype(F32)
        return total

    def start_gather(a, value):
        hid[a, core, x] = value.astype(BF16)
        each(NX, lambda k: g_copy(a, k).start())
        f_copy(a, 0).start()

    def next_gather(a):
        for k in (NX - 1, NX - 2, 1):
            g_come(a, k).wait_recv()
            f_copy(a, spread(k, NX)).start()

    def end_gather(a):
        for off in range(NX):
            f_come(a, off).wait_recv()

    def project_out(a, mat):
        left = dot(hid[a, 0].reshape(ROWS, HW), mat[pl.ds(PAD, TILE), :], 1, 1)
        right = dot(hid[a, 1].reshape(ROWS, HW), mat[pl.ds(0, TILE), :], 1, 1)
        cut = LANES - TILE
        return jnp.concatenate([left[:, :cut], left[:, cut:] + right[:, :TILE - cut], right[:, TILE - cut:]], axis=1)

    def weight_grad(a, h, out, hbm, sem):
        step = 256
        for n in range(HW // step):
            cols = pl.ds(n * step, step)
            left = dot(rows[a, :, pl.ds(0, TILE)], hid[h, 0, :, :, cols].reshape(ROWS, step), 0, 0)
            right = dot(rows[a, :, pl.ds(LANES - TILE, TILE)], hid[h, 1, :, :, cols].reshape(ROWS, step), 0, 0)
            grad_w[out, :, cols] = (left[:WIDTH] + right[PAD:]).astype(BF16)
        copy = pltpu.make_async_copy(grad_w.at[out], hbm, store_sem.at[out])
        copy.start()
        return copy

    def send_back(a, mat):
        send_y(project_out(a, mat), yb_out, yb_in, yb_send, yb_recv, a)

    def turn_back(a):
        got = take_y(yb_out, yb_in, yb_send, yb_recv, a)
        zb_out[a] = dot(perm_back[...], got).astype(BF16).reshape(NZ, 2 * NY, LANES)
        send_z(zb_out, zb_in, zb_send, zb_recv, a)

    def picked(a):
        got = take_z(zb_out, zb_in, zb_send, zb_recv, a)
        left = dot(got[:, :TILE], pick[0], 0, 0)
        right = dot(got[:, LANES - TILE:], pick[1], 0, 0)
        return left[:WIDTH] + right[PAD:]

    loads[0].wait()
    loads[1].wait()
    z_out[0] = dot(chosen, tok_src[...], 1, 1).astype(BF16).reshape(NZ, 2 * NY, LANES)
    pl.semaphore_wait(barrier, NZ + NY + NX + NCORE - 4)
    send_z(z_out, z_in, z_send, z_recv, 0)
    loads[2].wait()
    loads[3].wait()
    z_out[1] = (scale * dot(chosen, cot_src[...], 1, 1)).astype(BF16).reshape(NZ, 2 * NY, LANES)
    send_z(z_out, z_in, z_send, z_recv, 1)
    loads[4].wait()
    loads[5].wait()

    def turn(a):
        send_y(dot(perm_out[...], take_z(z_out, z_in, z_send, z_recv, a)), y_out, y_in, y_send, y_recv, a)

    turn(0)
    rows[0] = take_y(y_out, y_in, y_send, y_recv, 0)
    start_sum(0, gate_w)
    next_sum(0)
    turn(1)
    gate = end_sum(0)
    gate_keep[...] = gate
    start_gather(0, gate * jax.nn.sigmoid(gate))
    next_gather(0)
    end_gather(0)
    send_back(0, down_w)
    rows[1] = take_y(y_out, y_in, y_send, y_recv, 1)
    start_sum(1, down_w)
    next_sum(1)
    turn_back(0)
    wide = end_sum(1)
    gate = gate_keep[...]
    sig = jax.nn.sigmoid(gate)
    start_gather(1, wide * sig * (1.0 + gate * (1.0 - sig)))
    next_gather(1)
    end_gather(1)
    send_back(1, gate_w)
    stores = [weight_grad(0, 1, 0, gate_grad_hbm, store_sem)]
    turn_back(1)
    stores.append(weight_grad(1, 0, 1, down_grad_hbm, store_sem))
    both = picked(0)
    mixed_ref[...] = (both[:, :TOK] * weight_ref[0:1, :] + both[:, TOK:] * weight_ref[1:2, :]).astype(BF16)
    both = picked(1)
    grad_ref[...] = (both[:, :TOK] + both[:, TOK:]).astype(BF16)

    for a in range(2):
        each(NZ, lambda k: z_copy(z_out, z_in, z_send, z_recv, a, k).wait_send())
        each(NY, lambda k: y_copy(y_out, y_in, y_send, y_recv, a, k).wait_send())
        each(NX, lambda k: x_copy(a, k).wait_send())
        each(NX, lambda k: g_copy(a, k).wait_send())
        for off in range(NX):
            f_copy(a, off).wait_send()
        c_copy(a).wait_send()
        each(NY, lambda k: y_copy(yb_out, yb_in, yb_send, yb_recv, a, k).wait_send())
        each(NZ, lambda k: z_copy(zb_out, zb_in, zb_send, zb_recv, a, k).wait_send())
    for store in stores:
        store.wait()


def per_device(tokens, cotangent, slot_route, route_weight, w_gate, w_down):
    hbm, vmem = pl.BlockSpec(memory_space=pl.ANY), pl.BlockSpec(memory_space=pltpu.VMEM)
    dma = pltpu.SemaphoreType.DMA
    mixed, input_grad, gate_grad, down_grad = pl.pallas_call(
        layer,
        out_shape=(
            jax.ShapeDtypeStruct((WIDTH, TOK), BF16),
            jax.ShapeDtypeStruct((WIDTH, TOK), BF16),
            jax.ShapeDtypeStruct((WIDTH, HW), BF16),
            jax.ShapeDtypeStruct((WIDTH, HW), BF16),
        ),
        in_specs=[hbm, hbm, vmem, vmem, hbm, hbm],
        out_specs=(vmem, vmem, hbm, hbm),
        scratch_shapes=[
            pltpu.VMEM((LANES, 2 * TOK), BF16), pltpu.VMEM((LANES, 2 * TOK), BF16),
            pltpu.VMEM((WIDTH + 2 * PAD, HW), BF16), pltpu.VMEM((WIDTH + 2 * PAD, HW), BF16),
            pltpu.VMEM((2, ROWS, 2 * TOK), BF16),
            pltpu.VMEM((ROWS, ROWS), BF16), pltpu.VMEM((ROWS, ROWS), BF16),
            pltpu.VMEM((2, NZ, 2 * NY, LANES), BF16), pltpu.VMEM((2, NZ, 2 * NY, LANES), BF16),
            pltpu.VMEM((2, NY, 2 * NZ, LANES), BF16), pltpu.VMEM((2, NY, 2 * NZ, LANES), BF16),
            pltpu.VMEM((2, ROWS, LANES), BF16),
            pltpu.VMEM((2, ROWS, HW), BF16), pltpu.VMEM((2, ROWS, HW), BF16),
            pltpu.VMEM((2, ROWS, HW), F32),
            pltpu.VMEM((2, NX, PART, HW), BF16), pltpu.VMEM((2, NX, PART, HW), BF16),
            pltpu.VMEM((2, NCORE, NX, PART, HW), BF16),
            pltpu.VMEM((PART, HW), F32),
            pltpu.VMEM((2, NY, 2 * NZ, LANES), BF16), pltpu.VMEM((2, NY, 2 * NZ, LANES), BF16),
            pltpu.VMEM((2, NZ, 2 * NY, LANES), BF16), pltpu.VMEM((2, NZ, 2 * NY, LANES), BF16),
            pltpu.VMEM((2, WIDTH, HW), BF16),
            dma((6,)), dma((2,)),
            dma((2, NZ)), dma((2, NZ)), dma((2, NY)), dma((2, NY)), dma((2,)), dma((2,)),
            dma((2, NX)), dma((2, NX)), dma((2, NX)), dma((2, NX)), dma((2, NX)), dma((2, NX)),
            dma((2, NY)), dma((2, NY)), dma((2, NZ)), dma((2, NZ)),
        ],
        compiler_params=pltpu.CompilerParams(
            collective_id=0, has_side_effects=True, vmem_limit_bytes=48 * 1024 * 1024),
        name="moe_layer",
    )(tokens.T, cotangent.T, slot_route.T, route_weight.T, w_gate[0], w_down[0].T)
    return mixed.T, input_grad.T, gate_grad[None], down_grad.T[None]


def solution(mesh):
    return jax.shard_map(
        per_device,
        mesh=mesh,
        in_specs=(
            P("dp", "expert"),
            P("dp", "expert"),
            P("dp", None),
            P("dp", None),
            P("dp", "expert", None),
            P("dp", None, "expert"),
        ),
        out_specs=(
            P("dp", "expert"),
            P("dp", "expert"),
            P("dp", "expert", None),
            P("dp", None, "expert"),
        ),
        check_vma=False,
    )
```

time: 241 us -> 116 us (0.48)
  the two profiles are of different devices: /device:TPU:14 before, /device:TPU:1 now
where the time goes in v2:
time: 116 us; the launch traced here: 115 us
  Pallas kernels  107 us (92%)
  local copies, waits for them, and re-layouts  7.97 us (7%)
    pallas_call x1, Pallas kernels, per_device(): pl.pallas_call(layer, out_shape=(jax.ShapeDtypeStruct((WIDTH, TOK), BF16)...  107 us
    unnamed x16, local copies, waits for them, and re-layouts  7.97 us

profile of v2, /device:TPU:1, one launch (start us, length us, event | category | flops | bytes accessed | tf_op | source)
XLA Modules:
  0.0 115.3 jit_solution(1121254197317874990)
XLA Ops:
  0.6 0.0 copy-start.5
  0.6 0.0 copy-start.4
  0.7 0.7 copy-done.5
  1.3 0.0 copy-done.4
  1.3 0.0 copy-start
  1.3 1.2 %copy-done = bf16[1,448,1024]{2,1,0:T(8,128)(2,1)S(1)} copy-done((bf16[1,448,1024]{2,1,0:T(8,128)(2,1)S(1)}, bf16[1,448,1024]{2,1,0:T(8,128)(2,1)}, u32[]{:S(2)}) %copy-start) | copy-done | bytes 917528
  2.5 0.0 copy-start.1
  2.5 1.2 %copy-done.1 = bf16[1,1024,448]{1,2,0:T(8,128)(2,1)S(1)} copy-done((bf16[1,1024,448]{1,2,0:T(8,128)(2,1)S(1)}, bf16[1,1024,448]{1,2,0:T(8,128)(2,1)}, u32[]{:S(2)}) %copy-start.1) | copy-done | bytes 917528
  3.7 0.0 copy-start.2
  3.7 0.9 copy-done.2
  4.6 0.0 copy-start.3
  4.6 0.9 copy-done.3
  5.5 106.7 %moe_layer.1 = (bf16[448,128]{1,0:T(8,128)(2,1)S(1)}, bf16[448,128]{1,0:T(8,128)(2,1)S(1)}, bf16[448,1024]{1,0:T(8,128)(2,1)S(1)}, bf16[448,1024]{1,0:T(8,128)(2,1)S(1)}) custom-call(bf16[448,128]{1,0:T(8,128)(2,1)S(1)} %bitcast.20, bf16[448,128]{1,0:T(8,128)(2,1)S(1)} %bitcast.21, s32[2,128]{1,0:T(2,128)S(1)} %bitcast.22, f32[2,128]{1,0:T(2,128)S(1)} %bitcast.23, ...), custom_call_target="tpu_custom_call" | custom-call | tf_op jit(solution)/shard_map/moe_layer/pallas_call | solution.py:338
  112.2 0.6 copy.14
  112.8 0.6 copy.15
  113.5 0.9 copy.16
  114.4 0.9 copy.17
Async XLA Ops:
  0.6 0.7 copy-start.5
  0.6 0.7 copy-start.4
  1.3 1.2 %copy-start = (bf16[1,448,1024]{2,1,0:T(8,128)(2,1)S(1)}, bf16[1,448,1024]{2,1,0:T(8,128)(2,1)}, u32[]{:S(2)}) copy-start(bf16[1,448,1024]{2,1,0:T(8,128)(2,1)} %param.10) | copy-start | bytes 2752516
  2.5 1.2 %copy-start.1 = (bf16[1,1024,448]{1,2,0:T(8,128)(2,1)S(1)}, bf16[1,1024,448]{1,2,0:T(8,128)(2,1)}, u32[]{:S(2)}) copy-start(bf16[1,1024,448]{1,2,0:T(8,128)(2,1)} %param.11) | copy-start | bytes 2752516
  3.7 0.9 copy-start.2
  4.6 0.9 copy-start.3

commit v3 on v1

v3 whole, which is shorter than its diff:
```python
import jax
import jax.numpy as jnp
from jax import lax
from jax.experimental import pallas as pl
from jax.experimental.pallas import tpu as pltpu
from jax.sharding import PartitionSpec as P

NY, NZ, NX, NCORE = 8, 12, 4, 2
BF16, F32 = jnp.bfloat16, jnp.float32
MESH = pl.DeviceIdType.MESH
TOK = 128
WIDTH = 448
TILE = 512
LANES = 2 * WIDTH
ROWS = 2 * NY * NZ
HW = 1024
COLS = HW // NX
SETS = ((0, 3, 6, 9), (1, 5, 7, 11), (2, 4, 8, 10))
OFFSETS = SETS[0] + SETS[1] + SETS[2]
LEN = len(SETS[0])
CHUNK = ROWS // len(SETS)
UNITS = tuple((kind, chunk) for kind in range(2) for chunk in range(len(SETS)))
STEPS = (("turn", 0.0), ("sum", 4.0), ("sum_x", 6.2), ("act", 8.7), ("forward", 11.5), ("out", 12.3), ("back", 17.0))
BETWEEN = 3.7


def spread(k, n):
    return n // 2 + (k // 2) * (1 - 2 * (k % 2))


def dot(a, b, contract_a=1, contract_b=0):
    return lax.dot_general(a, b, (((contract_a,), (contract_b,)), ((), ())), preferred_element_type=F32)


def each(n, step):
    def one(k, carry):
        step(k)
        return carry

    lax.fori_loop(1, n, one, 0)


def layer(
    tok_hbm, cot_hbm, slot_ref, weight_ref, gate_hbm, down_hbm,
    mixed_ref, grad_ref, gate_grad_hbm, down_grad_hbm,
    tok_src, cot_src, gate_w, down_w, pick, perm_out, perm_back,
    z_out, z_in, y_out, y_in, rows,
    core_out, core_in, own, x_out, x_in, hid, gate_keep,
    yb_out, yb_in, zb_out, zb_in, weight_grads,
    load_sem, store_sem,
    z_send, z_recv, y_send, y_recv, c_send, c_recv, x_send, x_recv,
    g_send, g_recv, f_send, f_recv, yb_send, yb_recv, zb_send, zb_recv,
):
    dp, ex = lax.axis_index("dp"), lax.axis_index("expert")
    y, z = dp // NZ, dp % NZ
    x, core = ex // NCORE, ex % NCORE
    other = 1 - core
    mats = (gate_w, down_w)

    def at_z(off):
        return (y * NZ + (z + off) % NZ, ex)

    def at_y(k):
        return (((y + spread(k, NY)) % NY) * NZ + z, ex)

    def at_x(k):
        return (dp, ((x + spread(k, NX)) % NX) * NCORE + core)

    at_core = (dp, x * NCORE + other)

    barrier = pltpu.get_barrier_semaphore()

    def hello(to):
        pl.semaphore_signal(barrier, inc=1, device_id=to, device_id_type=MESH)

    each(NZ, lambda k: hello(at_z(k)))
    each(NY, lambda k: hello(at_y(k)))
    each(NX, lambda k: hello(at_x(k)))
    hello(at_core)

    loads = [
        pltpu.make_async_copy(tok_hbm, tok_src.at[pl.ds(0, WIDTH), pl.ds(0, TOK)], load_sem.at[0]),
        pltpu.make_async_copy(tok_hbm, tok_src.at[pl.ds(WIDTH, WIDTH), pl.ds(TOK, TOK)], load_sem.at[1]),
        pltpu.make_async_copy(cot_hbm, cot_src.at[pl.ds(0, WIDTH), pl.ds(0, TOK)], load_sem.at[2]),
        pltpu.make_async_copy(cot_hbm, cot_src.at[pl.ds(WIDTH, WIDTH), pl.ds(TOK, TOK)], load_sem.at[3]),
        pltpu.make_async_copy(gate_hbm, gate_w.at[pl.ds(0, WIDTH)], load_sem.at[4]),
        pltpu.make_async_copy(down_hbm, down_w.at[pl.ds(0, WIDTH)], load_sem.at[5]),
    ]
    for load in loads:
        load.start()

    for src in (tok_src, cot_src):
        src[pl.ds(0, WIDTH), pl.ds(TOK, TOK)] = jnp.zeros((WIDTH, TOK), BF16)
        src[pl.ds(WIDTH, WIDTH), pl.ds(0, TOK)] = jnp.zeros((WIDTH, TOK), BF16)

    inner = lax.broadcasted_iota(jnp.int32, (2 * NY, TOK), 0)
    to = jnp.concatenate([(inner >> 1) * NZ + (z + off) % NZ for off in OFFSETS], axis=0)
    odd = (lax.broadcasted_iota(jnp.int32, (ROWS, TOK), 0) & 1) == 1
    half = NY * NZ // 2
    slot = jnp.where(odd, 2 * jnp.where(to < half, to + half, to - half) + 1, 2 * to)
    is_0, is_1 = slot == slot_ref[0:1, :], slot == slot_ref[1:2, :]
    named = jnp.where(is_0 | is_1, 1.0, 0.0)
    earlier = lax.broadcasted_iota(jnp.int32, (TOK, TOK), 0) < lax.broadcasted_iota(jnp.int32, (TOK, TOK), 1)
    before = dot(named.astype(BF16), jnp.where(earlier, 1.0, 0.0).astype(BF16))
    first = jnp.where(before < 0.5, 1.0, 0.0)
    later = 1.0 - first
    chosen = jnp.concatenate([named * first, named * later], axis=1).astype(BF16)
    loads[0].wait()
    loads[1].wait()
    z_out[0] = dot(chosen, tok_src[...], 1, 1).astype(BF16).reshape(NZ, 2 * NY, LANES)
    pl.semaphore_wait(barrier, NZ + NY + NX + NCORE - 4)

    def z_copy(src, dst, send, recv, kind, q):
        return pltpu.make_async_remote_copy(
            src_ref=src.at[kind, q], dst_ref=dst.at[kind, q], send_sem=send.at[kind, q], recv_sem=recv.at[kind, q],
            device_id=at_z(OFFSETS[q]), device_id_type=MESH)

    def zb_copy(src, dst, send, recv, kind, q):
        return pltpu.make_async_remote_copy(
            src_ref=src.at[kind, q], dst_ref=dst.at[kind, q], send_sem=send.at[kind, q], recv_sem=recv.at[kind, q],
            device_id=at_z(NZ - OFFSETS[q]), device_id_type=MESH)

    def y_copy(src, dst, send, recv, u, k):
        off = spread(k, NY)
        return pltpu.make_async_remote_copy(
            src_ref=src.at[u[0], u[1], (y + off) % NY], dst_ref=dst.at[u[0], u[1], y], send_sem=send.at[u[0], u[1], off],
            recv_sem=recv.at[u[0], u[1], off], device_id=at_y(k), device_id_type=MESH)

    def y_come(src, dst, send, recv, u, k):
        off = spread(k, NY)
        return pltpu.make_async_remote_copy(
            src_ref=src.at[u[0], u[1], y], dst_ref=dst.at[u[0], u[1], (y + NY - off) % NY], send_sem=send.at[u[0], u[1], off],
            recv_sem=recv.at[u[0], u[1], off], device_id=at_y(k), device_id_type=MESH)

    def part(u):
        return pl.ds(u[1] * CHUNK, CHUNK)

    def hid_rows(u, position):
        return pl.ds(pl.multiple_of(u[1] * 2 * CHUNK + position * CHUNK, CHUNK), CHUNK)

    def x_copy(u, k):
        off = spread(k, NX)
        return pltpu.make_async_remote_copy(
            src_ref=x_out.at[u[0], (x + off) % NX, part(u)], dst_ref=x_in.at[u[0], x, part(u)], send_sem=x_send.at[u[0], u[1], off],
            recv_sem=x_recv.at[u[0], u[1], off], device_id=at_x(k), device_id_type=MESH)

    def x_come(u, k):
        off = spread(k, NX)
        return pltpu.make_async_remote_copy(
            src_ref=x_out.at[u[0], x, part(u)], dst_ref=x_in.at[u[0], (x + NX - off) % NX, part(u)], send_sem=x_send.at[u[0], u[1], off],
            recv_sem=x_recv.at[u[0], u[1], off], device_id=at_x(k), device_id_type=MESH)

    def g_copy(u, k):
        off = spread(k, NX)
        mine = hid.at[u[0], x, hid_rows(u, core)]
        return pltpu.make_async_remote_copy(
            src_ref=mine, dst_ref=mine, send_sem=g_send.at[u[0], u[1], off],
            recv_sem=g_recv.at[u[0], u[1], off], device_id=at_x(k), device_id_type=MESH)

    def g_come(u, k):
        off = spread(k, NX)
        return pltpu.make_async_remote_copy(
            src_ref=hid.at[u[0], x, hid_rows(u, core)], dst_ref=hid.at[u[0], (x + NX - off) % NX, hid_rows(u, core)],
            send_sem=g_send.at[u[0], u[1], off], recv_sem=g_recv.at[u[0], u[1], off], device_id=at_x(k), device_id_type=MESH)

    def f_copy(u, off):
        block = hid.at[u[0], (x + NX - off) % NX, hid_rows(u, core)]
        return pltpu.make_async_remote_copy(
            src_ref=block, dst_ref=block, send_sem=f_send.at[u[0], u[1], off],
            recv_sem=f_recv.at[u[0], u[1], off], device_id=at_core, device_id_type=MESH)

    def f_come(u, off):
        frm = (x + NX - off) % NX
        return pltpu.make_async_remote_copy(
            src_ref=hid.at[u[0], frm, hid_rows(u, core)], dst_ref=hid.at[u[0], frm, hid_rows(u, other)],
            send_sem=f_send.at[u[0], u[1], off], recv_sem=f_recv.at[u[0], u[1], off], device_id=at_core, device_id_type=MESH)

    def c_copy(u):
        return pltpu.make_async_remote_copy(
            src_ref=core_out.at[u[0], part(u)], dst_ref=core_in.at[u[0], part(u)], send_sem=c_send.at[u[0], u[1]],
            recv_sem=c_recv.at[u[0], u[1]], device_id=at_core, device_id_type=MESH)

    blocks = [[q for q in range(c * LEN, (c + 1) * LEN)] for c in range(len(SETS))]
    far = (NX - 1, NX - 2, 1)

    def send_z(u):
        for q in blocks[u[1]]:
            if OFFSETS[q]:
                z_copy(z_out, z_in, z_send, z_recv, u[0], q).start()
            else:
                z_in[u[0], q] = z_out[u[0], q]

    def send_y(value, src, dst, send, recv, u):
        src[u[0], u[1]] = value.reshape(NY, 2 * LEN, LANES).astype(BF16)
        each(NY, lambda k: y_copy(src, dst, send, recv, u, k).start())
        dst[u[0], u[1], y] = src[u[0], u[1], y]

    def take_y(src, dst, send, recv, u):
        each(NY, lambda k: y_come(src, dst, send, recv, u, k).wait_recv())
        return dst[u[0], u[1]].astype(F32).reshape(CHUNK, LANES)

    def turn(u):
        for q in blocks[u[1]]:
            if OFFSETS[q]:
                z_copy(z_out, z_in, z_send, z_recv, u[0], q).wait_recv()
        got = z_in[u[0], pl.ds(u[1] * LEN, LEN)].reshape(CHUNK, LANES)
        send_y(dot(perm_out[...], got), y_out, y_in, y_send, y_recv, u)

    def partial_sum(u):
        got = take_y(y_out, y_in, y_send, y_recv, u)
        right = pltpu.roll(got[:, LANES - TILE:], WIDTH, 1)
        both = jnp.concatenate([got[:, :TILE], right], axis=0).astype(BF16)
        rows[u[0], pl.ds(u[1] * 2 * CHUNK, 2 * CHUNK)] = both
        total = dot(both, mats[u[0]][...])
        low, high = total[:CHUNK], total[CHUNK:]
        core_out[u[0], part(u)] = jnp.where(core == 0, high, low).astype(BF16)
        c_copy(u).start()
        own[u[0], part(u)] = jnp.where(core == 0, low, high)

    def sum_x(u):
        c_copy(u).wait_recv()
        total = own[u[0], part(u)] + core_in[u[0], part(u)].astype(F32)
        own[u[0], part(u)] = total
        for i in range(NX):
            x_out[u[0], i, part(u)] = total[:, i * COLS:(i + 1) * COLS].astype(BF16)
        each(NX, lambda k: x_copy(u, k).start())

    def act(u):
        each(NX, lambda k: x_come(u, k).wait_recv())
        total = own[u[0], part(u), pl.ds(pl.multiple_of(x * COLS, COLS), COLS)]
        for off in range(1, NX):
            total = total + x_in[u[0], (x + NX - off) % NX, part(u)].astype(F32)
        if u[0] == 0:
            gate_keep[part(u)] = total
            value = total * jax.nn.sigmoid(total)
        else:
            gate = gate_keep[part(u)]
            sig = jax.nn.sigmoid(gate)
            value = total * sig * (1.0 + gate * (1.0 - sig))
        hid[u[0], x, hid_rows(u, core)] = value.astype(BF16)
        each(NX, lambda k: g_copy(u, k).start())
        f_copy(u, 0).start()

    def forward(u):
        for k in far:
            g_come(u, k).wait_recv()
            f_copy(u, spread(k, NX)).start()

    def out(u):
        for off in range(NX):
            f_come(u, off).wait_recv()
        both = pl.ds(u[1] * 2 * CHUNK, 2 * CHUNK)
        value = jnp.concatenate([hid[u[0], i, both] for i in range(NX)], axis=1)
        value = dot(value, mats[1 - u[0]][...], 1, 1)
        left, right = value[:CHUNK], pltpu.roll(value[CHUNK:], TILE - WIDTH, 1)
        cut = LANES - TILE
        value = jnp.concatenate([left[:, :cut], left[:, cut:] + right[:, :TILE - cut], right[:, TILE - cut:]], axis=1)
        send_y(value, yb_out, yb_in, yb_send, yb_recv, u)

    def back(u):
        got = take_y(yb_out, yb_in, yb_send, yb_recv, u).astype(BF16)
        zb_out[u[0], pl.ds(u[1] * LEN, LEN)] = dot(perm_back[...], got).astype(BF16).reshape(LEN, 2 * NY, LANES)
        for q in blocks[u[1]]:
            if OFFSETS[q]:
                zb_copy(zb_out, zb_in, zb_send, zb_recv, u[0], q).start()
            else:
                zb_in[u[0], q] = zb_out[u[0], q]

    def picked(kind, c, n):
        for q in range(c * LEN, (c + n) * LEN):
            if OFFSETS[q]:
                zb_copy(zb_out, zb_in, zb_send, zb_recv, kind, q).wait_recv()
        got = zb_in[kind, pl.ds(c * LEN, n * LEN)].reshape(n * CHUNK, LANES)
        here = pl.ds(c * CHUNK, n * CHUNK)
        left = dot(got[:, :TILE], pick[0, here], 0, 0)
        right = dot(got[:, LANES - TILE:], pick[1, here], 0, 0)
        return left[:WIDTH] + right[TILE - WIDTH:]

    stores = [
        pltpu.make_async_copy(weight_grads.at[kind], result, store_sem.at[kind])
        for kind, result in enumerate((gate_grad_hbm, down_grad_hbm))]

    def weight_grad(kind):
        for i in range(NX):
            grad = dot(rows[kind], hid[1 - kind, i], 0, 0)
            weight_grads[kind, :, pl.ds(i * COLS, COLS)] = grad[:WIDTH].astype(BF16)
        stores[kind].start()

    send_z(UNITS[0])
    send_z(UNITS[1])
    one_0, one_1 = jnp.where(is_0, 1.0, 0.0), jnp.where(is_1, 1.0, 0.0)
    weight_of = one_0 * weight_ref[0:1, :] + one_1 * weight_ref[1:2, :]
    scale_first = jnp.sum(weight_of * first, axis=1, keepdims=True)
    scale_later = jnp.sum(weight_of * later, axis=1, keepdims=True)
    lane = lax.broadcasted_iota(jnp.int32, (ROWS, LANES), 1)
    scale = jnp.where(lane < WIDTH, scale_first, scale_later)
    loads[2].wait()
    loads[3].wait()
    z_out[1] = (scale * dot(chosen, cot_src[...], 1, 1)).astype(BF16).reshape(NZ, 2 * NY, LANES)
    pick[0] = jnp.concatenate([one_0 * first, one_1 * first], axis=1).astype(BF16)
    pick[1] = jnp.concatenate([one_0 * later, one_1 * later], axis=1).astype(BF16)
    down_axis = lax.broadcasted_iota(jnp.int32, (CHUNK, CHUNK), 0)
    along_axis = lax.broadcasted_iota(jnp.int32, (CHUNK, CHUNK), 1)

    def place(c):
        return ((c >> 1) & (NY - 1)) * (2 * LEN) + (c >> 4) * 2 + (c & 1)

    perm_out[...] = jnp.where(down_axis == place(along_axis), 1.0, 0.0).astype(BF16)
    perm_back[...] = jnp.where(place(down_axis) == along_axis, 1.0, 0.0).astype(BF16)
    for mat in mats:
        mat[pl.ds(WIDTH, TILE - WIDTH), :] = jnp.zeros((TILE - WIDTH, HW), BF16)
    loads[4].wait()
    loads[5].wait()

    names = dict(turn=turn, sum=partial_sum, sum_x=sum_x, act=act, forward=forward, out=out, back=back)
    plan = sorted(
        ((n * BETWEEN + at, n, name) for n in range(len(UNITS)) for name, at in STEPS), key=lambda e: e[:2])
    for _, n, name in plan:
        if name == "turn" and n + 2 < len(UNITS):
            send_z(UNITS[n + 2])
        names[name](UNITS[n])
        if name == "out" and n == len(UNITS) - 1:
            weight_grad(1)
    weight_grad(0)
    both = picked(0, 0, len(SETS))
    mixed_ref[...] = (both[:, :TOK] * weight_ref[0:1, :] + both[:, TOK:] * weight_ref[1:2, :]).astype(BF16)
    both = picked(1, 0, len(SETS) - 1)
    both = both + picked(1, len(SETS) - 1, 1)
    grad_ref[...] = (both[:, :TOK] + both[:, TOK:]).astype(BF16)

    for u in UNITS:
        for q in blocks[u[1]]:
            if OFFSETS[q]:
                z_copy(z_out, z_in, z_send, z_recv, u[0], q).wait_send()
                zb_copy(zb_out, zb_in, zb_send, zb_recv, u[0], q).wait_send()
        each(NY, lambda k: y_copy(y_out, y_in, y_send, y_recv, u, k).wait_send())
        each(NY, lambda k: y_copy(yb_out, yb_in, yb_send, yb_recv, u, k).wait_send())
        each(NX, lambda k: x_copy(u, k).wait_send())
        each(NX, lambda k: g_copy(u, k).wait_send())
        for off in range(NX):
            f_copy(u, off).wait_send()
        c_copy(u).wait_send()
    for store in stores:
        store.wait()


def write(*refs):
    n = len(refs) // 2
    copies = [pltpu.make_async_copy(refs[i], refs[n + i], refs[2 * n].at[i]) for i in range(n)]
    for copy in copies:
        copy.start()
    for copy in copies:
        copy.wait()


def per_device(tokens, cotangent, slot_route, route_weight, w_gate, w_down):
    hbm, vmem = pl.BlockSpec(memory_space=pltpu.HBM), pl.BlockSpec(memory_space=pltpu.VMEM)
    dma = pltpu.SemaphoreType.DMA
    chunks = len(SETS)
    shapes = (
        jax.ShapeDtypeStruct((WIDTH, TOK), BF16),
        jax.ShapeDtypeStruct((WIDTH, TOK), BF16),
        jax.ShapeDtypeStruct((WIDTH, HW), BF16),
        jax.ShapeDtypeStruct((WIDTH, HW), BF16),
    )
    results = pl.pallas_call(
        layer,
        out_shape=shapes,
        in_specs=[hbm, hbm, vmem, vmem, hbm, hbm],
        out_specs=(vmem, vmem, hbm, hbm),
        scratch_shapes=[
            pltpu.VMEM((LANES, 2 * TOK), BF16), pltpu.VMEM((LANES, 2 * TOK), BF16),
            pltpu.VMEM((TILE, HW), BF16), pltpu.VMEM((TILE, HW), BF16),
            pltpu.VMEM((2, ROWS, 2 * TOK), BF16),
            pltpu.VMEM((CHUNK, CHUNK), BF16), pltpu.VMEM((CHUNK, CHUNK), BF16),
            pltpu.VMEM((2, NZ, 2 * NY, LANES), BF16), pltpu.VMEM((2, NZ, 2 * NY, LANES), BF16),
            pltpu.VMEM((2, chunks, NY, 2 * LEN, LANES), BF16), pltpu.VMEM((2, chunks, NY, 2 * LEN, LANES), BF16),
            pltpu.VMEM((2, 2 * ROWS, TILE), BF16),
            pltpu.VMEM((2, ROWS, HW), BF16), pltpu.VMEM((2, ROWS, HW), BF16),
            pltpu.VMEM((2, ROWS, HW), F32),
            pltpu.VMEM((2, NX, ROWS, COLS), BF16), pltpu.VMEM((2, NX, ROWS, COLS), BF16),
            pltpu.VMEM((2, NX, 2 * ROWS, COLS), BF16),
            pltpu.VMEM((ROWS, COLS), F32),
            pltpu.VMEM((2, chunks, NY, 2 * LEN, LANES), BF16), pltpu.VMEM((2, chunks, NY, 2 * LEN, LANES), BF16),
            pltpu.VMEM((2, NZ, 2 * NY, LANES), BF16), pltpu.VMEM((2, NZ, 2 * NY, LANES), BF16),
            pltpu.VMEM((2, WIDTH, HW), BF16),
            dma((6,)), dma((2,)),
            dma((2, NZ)), dma((2, NZ)), dma((2, chunks, NY)), dma((2, chunks, NY)), dma((2, chunks)), dma((2, chunks)),
            dma((2, chunks, NX)), dma((2, chunks, NX)), dma((2, chunks, NX)), dma((2, chunks, NX)),
            dma((2, chunks, NX)), dma((2, chunks, NX)),
            dma((2, chunks, NY)), dma((2, chunks, NY)), dma((2, NZ)), dma((2, NZ)),
        ],
        compiler_params=pltpu.CompilerParams(
            collective_id=0, has_side_effects=True, vmem_limit_bytes=58 * 1024 * 1024),
        name="moe_layer",
    )(tokens.T, cotangent.T, slot_route.T, route_weight.T, w_gate[0], w_down[0].T)
    mixed, input_grad, gate_grad, down_grad = pl.pallas_call(
        write,
        out_shape=shapes,
        in_specs=[vmem] * 4,
        out_specs=(hbm,) * 4,
        scratch_shapes=[dma((4,))],
        name="write_results",
    )(*results)
    return mixed.T, input_grad.T, gate_grad[None], down_grad.T[None]


def solution(mesh):
    return jax.shard_map(
        per_device,
        mesh=mesh,
        in_specs=(
            P("dp", "expert"),
            P("dp", "expert"),
            P("dp", None),
            P("dp", None),
            P("dp", "expert", None),
            P("dp", None, "expert"),
        ),
        out_specs=(
            P("dp", "expert"),
            P("dp", "expert"),
            P("dp", "expert", None),
            P("dp", None, "expert"),
        ),
        check_vma=False,
    )
```

time: 241 us -> 98.2 us (0.41)
  the two profiles are of different devices: /device:TPU:14 before, /device:TPU:1 now
where the time goes in v3:
time: 98.2 us; the launch traced here: 98 us
  Pallas kernels  97.3 us (99%)
    pallas_call x1, Pallas kernels, per_device(): pl.pallas_call(layer, out_shape=shapes, in_specs=[hbm, hbm, vmem, vmem, h...  94.4 us
    pallas_call x1, Pallas kernels, per_device(): pl.pallas_call(write, out_shape=shapes, in_specs=[vmem] * 4, out_specs=(h...  2.92 us

profile of v3, /device:TPU:1, one launch (start us, length us, event | category | flops | bytes accessed | tf_op | source)
XLA Modules:
  0.0 98.0 jit_solution(602759359167454339)
XLA Ops:
  0.6 94.4 %moe_layer.1 = (bf16[448,128]{1,0:T(8,128)(2,1)}, bf16[448,128]{1,0:T(8,128)(2,1)}, bf16[448,1024]{1,0:T(8,128)(2,1)}, bf16[448,1024]{1,0:T(8,128)(2,1)}) custom-call(bf16[448,128]{1,0:T(8,128)(2,1)} %bitcast.16, bf16[448,128]{1,0:T(8,128)(2,1)} %bitcast.17, s32[2,128]{1,0:T(2,128)} %bitcast.18, f32[2,128]{1,0:T(2,128)} %bitcast.19, ...), custom_call_target="tpu_custom_call" | custom-call | tf_op jit(solution)/shard_map/moe_layer/pallas_call | solution.py:366
  95.1 2.9 %write_results.1 = (bf16[448,128]{1,0:T(8,128)(2,1)}, bf16[448,128]{1,0:T(8,128)(2,1)}, bf16[448,1024]{1,0:T(8,128)(2,1)}, bf16[448,1024]{1,0:T(8,128)(2,1)}) custom-call(bf16[448,128]{1,0:T(8,128)(2,1)} %get-tuple-element.12.refs_0_, bf16[448,128]{1,0:T(8,128)(2,1)} %get-tuple-element.13.refs_1_, bf16[448,1024]{1,0:T(8,128)(2,1)} %get-tuple-element.14.refs_2_, ...), custom_call_target="tpu_custom_call" | custom-call | tf_op jit(solution)/shard_map/write_results/pallas_call | solution.py:397

commit v4 on v3

--- a/solution.py
+++ b/solution.py
@@ -20,7 +20,7 @@
 LEN = len(SETS[0])
 CHUNK = ROWS // len(SETS)
 UNITS = tuple((kind, chunk) for kind in range(2) for chunk in range(len(SETS)))
-STEPS = (("turn", 0.0), ("sum", 4.0), ("sum_x", 6.2), ("act", 8.7), ("forward", 11.5), ("out", 12.3), ("back", 17.0))
+STEPS = (("turn", 0.0), ("sum", 8.5), ("sum_x", 11.0), ("act", 15.5), ("forward", 20.0), ("out", 22.0), ("back", 30.0))
 BETWEEN = 3.7
 
 
@@ -33,11 +33,8 @@
 
 
 def each(n, step):
-    def one(k, carry):
+    for k in range(1, n):
         step(k)
-        return carry
-
-    lax.fori_loop(1, n, one, 0)
 
 
 def layer(
@@ -163,17 +160,16 @@
             src_ref=hid.at[u[0], x, hid_rows(u, core)], dst_ref=hid.at[u[0], (x + NX - off) % NX, hid_rows(u, core)],
             send_sem=g_send.at[u[0], u[1], off], recv_sem=g_recv.at[u[0], u[1], off], device_id=at_x(k), device_id_type=MESH)
 
-    def f_copy(u, off):
-        block = hid.at[u[0], (x + NX - off) % NX, hid_rows(u, core)]
-        return pltpu.make_async_remote_copy(
-            src_ref=block, dst_ref=block, send_sem=f_send.at[u[0], u[1], off],
-            recv_sem=f_recv.at[u[0], u[1], off], device_id=at_core, device_id_type=MESH)
-
-    def f_come(u, off):
-        frm = (x + NX - off) % NX
-        return pltpu.make_async_remote_copy(
-            src_ref=hid.at[u[0], frm, hid_rows(u, core)], dst_ref=hid.at[u[0], frm, hid_rows(u, other)],
-            send_sem=f_send.at[u[0], u[1], off], recv_sem=f_recv.at[u[0], u[1], off], device_id=at_core, device_id_type=MESH)
+    def f_copy(u):
+        block = hid.at[u[0], :, hid_rows(u, core)]
+        return pltpu.make_async_remote_copy(
+            src_ref=block, dst_ref=block, send_sem=f_send.at[u[0], u[1]],
+            recv_sem=f_recv.at[u[0], u[1]], device_id=at_core, device_id_type=MESH)
+
+    def f_come(u):
+        return pltpu.make_async_remote_copy(
+            src_ref=hid.at[u[0], :, hid_rows(u, core)], dst_ref=hid.at[u[0], :, hid_rows(u, other)],
+            send_sem=f_send.at[u[0], u[1]], recv_sem=f_recv.at[u[0], u[1]], device_id=at_core, device_id_type=MESH)
 
     def c_copy(u):
         return pltpu.make_async_remote_copy(
@@ -239,16 +235,14 @@
             value = total * sig * (1.0 + gate * (1.0 - sig))
         hid[u[0], x, hid_rows(u, core)] = value.astype(BF16)
         each(NX, lambda k: g_copy(u, k).start())
-        f_copy(u, 0).start()
 
     def forward(u):
         for k in far:
             g_come(u, k).wait_recv()
-            f_copy(u, spread(k, NX)).start()
+        f_copy(u).start()
 
     def out(u):
-        for off in range(NX):
-            f_come(u, off).wait_recv()
+        f_come(u).wait_recv()
         both = pl.ds(u[1] * 2 * CHUNK, 2 * CHUNK)
         value = jnp.concatenate([hid[u[0], i, both] for i in range(NX)], axis=1)
         value = dot(value, mats[1 - u[0]][...], 1, 1)
@@ -316,9 +310,9 @@
     plan = sorted(
         ((n * BETWEEN + at, n, name) for n in range(len(UNITS)) for name, at in STEPS), key=lambda e: e[:2])
     for _, n, name in plan:
+        names[name](UNITS[n])
         if name == "turn" and n + 2 < len(UNITS):
             send_z(UNITS[n + 2])
-        names[name](UNITS[n])
         if name == "out" and n == len(UNITS) - 1:
             weight_grad(1)
     weight_grad(0)
@@ -337,8 +331,7 @@
         each(NY, lambda k: y_copy(yb_out, yb_in, yb_send, yb_recv, u, k).wait_send())
         each(NX, lambda k: x_copy(u, k).wait_send())
         each(NX, lambda k: g_copy(u, k).wait_send())
-        for off in range(NX):
-            f_copy(u, off).wait_send()
+        f_copy(u).wait_send()
         c_copy(u).wait_send()
     for store in stores:
         store.wait()
@@ -387,7 +380,7 @@
             dma((6,)), dma((2,)),
             dma((2, NZ)), dma((2, NZ)), dma((2, chunks, NY)), dma((2, chunks, NY)), dma((2, chunks)), dma((2, chunks)),
             dma((2, chunks, NX)), dma((2, chunks, NX)), dma((2, chunks, NX)), dma((2, chunks, NX)),
-            dma((2, chunks, NX)), dma((2, chunks, NX)),
+            dma((2, chunks)), dma((2, chunks)),
             dma((2, chunks, NY)), dma((2, chunks, NY)), dma((2, NZ)), dma((2, NZ)),
         ],
         compiler_params=pltpu.CompilerParams(

time: 98.2 us -> 90.5 us (0.922)
  Pallas kernels: 97.3 us -> 89.5 us
    pallas_call x1, Pallas kernels: 94.4 us -> 86.6 us  [per_device(): pl.pallas_call(layer, out_shape=shapes, in_specs=[hbm, hbm, vmem, vmem, h...]
where the time goes in v4:
time: 90.5 us; the launch traced here: 90.2 us
  Pallas kernels  89.5 us (99%)
    pallas_call x1, Pallas kernels, per_device(): pl.pallas_call(layer, out_shape=shapes, in_specs=[hbm, hbm, vmem, vmem, h...  86.6 us
    pallas_call x1, Pallas kernels, per_device(): pl.pallas_call(write, out_shape=shapes, in_specs=[vmem] * 4, out_specs=(h...  2.92 us

profile of v4, /device:TPU:1, one launch (start us, length us, event | category | flops | bytes accessed | tf_op | source)
XLA Modules:
  0.0 90.2 jit_solution(16005354559879911096)
XLA Ops:
  0.6 86.6 %moe_layer.1 = (bf16[448,128]{1,0:T(8,128)(2,1)}, bf16[448,128]{1,0:T(8,128)(2,1)}, bf16[448,1024]{1,0:T(8,128)(2,1)}, bf16[448,1024]{1,0:T(8,128)(2,1)}) custom-call(bf16[448,128]{1,0:T(8,128)(2,1)} %bitcast.16, bf16[448,128]{1,0:T(8,128)(2,1)} %bitcast.17, s32[2,128]{1,0:T(2,128)} %bitcast.18, f32[2,128]{1,0:T(2,128)} %bitcast.19, ...), custom_call_target="tpu_custom_call" | custom-call | tf_op jit(solution)/shard_map/moe_layer/pallas_call | solution.py:359
  87.2 2.9 %write_results.1 = (bf16[448,128]{1,0:T(8,128)(2,1)}, bf16[448,128]{1,0:T(8,128)(2,1)}, bf16[448,1024]{1,0:T(8,128)(2,1)}, bf16[448,1024]{1,0:T(8,128)(2,1)}) custom-call(bf16[448,128]{1,0:T(8,128)(2,1)} %get-tuple-element.12.refs_0_, bf16[448,128]{1,0:T(8,128)(2,1)} %get-tuple-element.13.refs_1_, bf16[448,1024]{1,0:T(8,128)(2,1)} %get-tuple-element.14.refs_2_, ...), custom_call_target="tpu_custom_call" | custom-call | tf_op jit(solution)/shard_map/write_results/pallas_call | solution.py:390

commit v5 on v4

--- a/solution.py
+++ b/solution.py
@@ -15,12 +15,12 @@
 ROWS = 2 * NY * NZ
 HW = 1024
 COLS = HW // NX
-SETS = ((0, 3, 6, 9), (1, 5, 7, 11), (2, 4, 8, 10))
+SETS = ((1, 5, 7, 11), (2, 4, 8, 10), (0, 3, 6, 9))
 OFFSETS = SETS[0] + SETS[1] + SETS[2]
 LEN = len(SETS[0])
 CHUNK = ROWS // len(SETS)
 UNITS = tuple((kind, chunk) for kind in range(2) for chunk in range(len(SETS)))
-STEPS = (("turn", 0.0), ("sum", 8.5), ("sum_x", 11.0), ("act", 15.5), ("forward", 20.0), ("out", 22.0), ("back", 30.0))
+STEPS = (("turn", 0.0), ("sum", 7.0), ("sum_x", 9.5), ("act", 14.0), ("forward", 18.5), ("out", 20.5), ("back", 28.5))
 BETWEEN = 3.7
 
 

time: 90.5 us -> 89.7 us (level)
  no operation moved by 1% of the time
where the time goes in v5:
time: 89.7 us; the launch traced here: 89.4 us
  Pallas kernels  88.8 us (99%)
    pallas_call x1, Pallas kernels, per_device(): pl.pallas_call(layer, out_shape=shapes, in_specs=[hbm, hbm, vmem, vmem, h...  85.9 us
    pallas_call x1, Pallas kernels, per_device(): pl.pallas_call(write, out_shape=shapes, in_specs=[vmem] * 4, out_specs=(h...  2.92 us

profile of v5, /device:TPU:1, one launch (start us, length us, event | category | flops | bytes accessed | tf_op | source)
XLA Modules:
  0.0 89.4 jit_solution(18247889664875071556)
XLA Ops:
  0.6 85.9 %moe_layer.1 = (bf16[448,128]{1,0:T(8,128)(2,1)}, bf16[448,128]{1,0:T(8,128)(2,1)}, bf16[448,1024]{1,0:T(8,128)(2,1)}, bf16[448,1024]{1,0:T(8,128)(2,1)}) custom-call(bf16[448,128]{1,0:T(8,128)(2,1)} %bitcast.16, bf16[448,128]{1,0:T(8,128)(2,1)} %bitcast.17, s32[2,128]{1,0:T(2,128)} %bitcast.18, f32[2,128]{1,0:T(2,128)} %bitcast.19, ...), custom_call_target="tpu_custom_call" | custom-call | tf_op jit(solution)/shard_map/moe_layer/pallas_call | solution.py:359
  86.5 2.9 %write_results.1 = (bf16[448,128]{1,0:T(8,128)(2,1)}, bf16[448,128]{1,0:T(8,128)(2,1)}, bf16[448,1024]{1,0:T(8,128)(2,1)}, bf16[448,1024]{1,0:T(8,128)(2,1)}) custom-call(bf16[448,128]{1,0:T(8,128)(2,1)} %get-tuple-element.12.refs_0_, bf16[448,128]{1,0:T(8,128)(2,1)} %get-tuple-element.13.refs_1_, bf16[448,1024]{1,0:T(8,128)(2,1)} %get-tuple-element.14.refs_2_, ...), custom_call_target="tpu_custom_call" | custom-call | tf_op jit(solution)/shard_map/write_results/pallas_call | solution.py:390
